TPU v7x, 256 devices: a whole 4x4x8 slice. The times are simulated.
256 devices in a mesh: row: 16 (over x, z_lo, core), col: 16 (over y, z_hi).
Axes of the slice: x: 4, y: 4, z: 8 (z_hi: 4, z_lo: 2; z = z_hi * 2 + z_lo), core: 2. Of those that a mesh axis runs over, the one named last changes fastest.
Arguments:
- velocity: float32 [3, 128, 256, 1536], P(None, 'col', None, 'row'), may hold values from -6 to 6
- dx_matrix: float32 [256, 256], replicated, may hold values from -0.375 to 0.375
- dy_matrix: float32 [1536, 1536], replicated, may hold values from -0.15625 to 0.15625
- dz_matrix: float32 [128, 128], replicated, may hold values from -0.5 to 0.5
- metric: float32 [1536], replicated, may hold values from 0.5 to 2
Outputs:
- convective: float32 [3, 128, 256, 1536], P(None, None, 'row', 'col')
All inputs are finite; a program needn't handle non-finite values.
Results may differ from a plain program's by a relative error of at most 0.000092.
Values sent between devices are 32-bit elements; how exact they have to be, the bound alone decides.
No kernel may reach another device: no remote copies, remote signals or barrier semaphores. Data moves between devices by JAX's collectives and lax.ppermute only.
A program may use at most 128 MiB of HBM per device.

v0:
```python
import jax
import jax.numpy as jnp
from jax import lax
from jax.sharding import PartitionSpec as P


def per_device(velocity, dx_matrix, dy_matrix, dz_matrix, metric):
    high = lax.Precision.HIGHEST
    deriv_x = jnp.einsum("czxy,Xx->czXy", velocity, dx_matrix, precision=high)
    partial_value = velocity[0][None] * deriv_x
    fields_y, partial_y = (
        lax.all_to_all(velocity, "row", split_axis=2, concat_axis=3, tiled=True),
        lax.all_to_all(partial_value, "row", split_axis=2, concat_axis=3, tiled=True),
    )
    deriv_y = jnp.einsum("czxy,Yy->czxY", fields_y, dy_matrix, precision=high) * metric
    accum = partial_y + fields_y[1][None] * deriv_y
    fields_z, accum_z = (
        lax.all_to_all(fields_y, "col", split_axis=3, concat_axis=1, tiled=True),
        lax.all_to_all(accum, "col", split_axis=3, concat_axis=1, tiled=True),
    )
    deriv_z = jnp.einsum("czxy,Zz->cZxy", fields_z, dz_matrix, precision=high)
    return accum_z + fields_z[2][None] * deriv_z


def solution(mesh):
    return jax.shard_map(
        per_device,
        mesh=mesh,
        in_specs=(P(None, "col", None, "row"), P(), P(), P(), P()),
        out_specs=P(None, None, "row", "col"),
        check_vma=False,
    )
```

profile of v0, /device:TPU:4, one launch (start us, length us, event | category | flops | bytes accessed | tf_op | source)
XLA Modules:
  0.0 315.5 jit_solution(9147374327070340412)
XLA Ops:
  3.4 6.2 %all-to-all-start.1 = ((f32[3,8,256,96]{3,1,0,2:T(8,128)}), f32[3,8,256,96]{3,1,0,2:T(8,128)S(1)}, u32[]{:S(2)}, u32[]{:S(2)}) async-start(f32[3,8,256,96]{3,1,0,2:T(8,128)} %copy.32), calls=%async_computation.1 | async-start | bytes 6291456 | tf_op jit(solution)/shard_map/all_to_all | solution.py:12
  10.8 5.3 %bitcast_multiply_fusion = f32[3,8,256,96]{2,3,1,0:T(8,128)} fusion(f32[3,8,256,96]{2,3,1,0:T(8,128)} %param.5, f32[8,256,96]{1,2,0:T(8,128)S(1)} %slice_bitcast_fusion, f32[256,256]{1,0:T(8,128)S(1)} %copy-done), kind=kOutput, calls=%fused_computation.6 | convolution fusion | flops 1812529152 | bytes 5767168 | tf_op jit(solution)/shard_map/czxy,Xx->czXy/dot_general | solution.py:9
  19.5 26.7 %all-to-all-done.1 = f32[3,8,256,96]{3,1,0,2:T(8,128)S(1)} async-done(((f32[3,8,256,96]{3,1,0,2:T(8,128)}), f32[3,8,256,96]{3,1,0,2:T(8,128)S(1)}, u32[]{:S(2)}, u32[]{:S(2)}) %all-to-all-start.1) | async-done | bytes 2359328 | tf_op jit(solution)/shard_map/all_to_all | solution.py:12
  46.2 7.2 %all-to-all-start = ((f32[3,8,256,96]{3,1,0,2:T(8,128)}), f32[3,8,256,96]{3,1,0,2:T(8,128)}, u32[]{:S(2)}, u32[]{:S(2)}) async-start(f32[3,8,256,96]{3,1,0,2:T(8,128)} %copy.29), calls=%async_computation | async-start | bytes 6291456 | tf_op jit(solution)/shard_map/all_to_all | solution.py:13
  56.9 4.4 %all_to_all.59 = f32[3,8,16,1536]{3,2,1,0:T(8,128)} reshape(f32[3,8,16,16,96]{4,3,2,1,0:T(8,128)} %copy.35) | data formatting | bytes 4718592 | tf_op jit(solution)/shard_map/all_to_all | solution.py:12
  62.7 27.2 %all-to-all-done = f32[3,8,256,96]{3,1,0,2:T(8,128)} async-done(((f32[3,8,256,96]{3,1,0,2:T(8,128)}), f32[3,8,256,96]{3,1,0,2:T(8,128)}, u32[]{:S(2)}, u32[]{:S(2)}) %all-to-all-start) | async-done | bytes 2359328 | tf_op jit(solution)/shard_map/all_to_all | solution.py:13
  89.9 5.4 %copy.31 = f32[3,8,16,16,96]{4,3,2,1,0:T(8,128)} copy(f32[3,8,16,16,96]{4,1,0,2,3:T(8,128)} %bitcast.6) | data formatting | bytes 4718592 | tf_op jit(solution)/shard_map/all_to_all | solution.py:13
  95.3 4.5 %all_to_all.55 = f32[3,8,16,1536]{3,2,1,0:T(8,128)} reshape(f32[3,8,16,16,96]{4,3,2,1,0:T(8,128)} %copy.31) | data formatting | bytes 4718592 | tf_op jit(solution)/shard_map/all_to_all | solution.py:13
  99.8 15.0 %fusion.8 = f32[3,8,16,1536]{3,2,1,0:T(8,128)} fusion(f32[3,8,16,1536]{3,2,1,0:T(8,128)} %all_to_all.55, f32[3,8,16,1536]{3,2,1,0:T(8,128)S(1)} %copy-done.2, f32[1536,1536]{1,0:T(8,128)} %param.7, f32[1536]{0:T(1024)S(1)} %copy-done.4, f32[8,16,1536]{2,1,0:T(8,128)S(1)} %mul.44), kind=kOutput, calls=%fused_computation.4 | convolution fusion | flops 10873405440 | bytes 17307648 | tf_op jit(solution)/shard_map/czxy,Yy->czxY/dot_general | solution.py:15
  114.8 11.4 %copy.36 = f32[3,8,16,1536]{2,1,0,3:T(8,128)} copy(f32[3,8,16,1536]{3,2,1,0:T(8,128)} %fusion.8) | data formatting | bytes 4718592 | tf_op jit(solution)/shard_map/add | solution.py:16
  126.2 15.9 %reshape.9 = f32[16,1,36864]{2,1,0:T(1,128)} reshape(f32[1536,3,8,16]{3,2,1,0:T(8,128)} %bitcast.56) | data formatting | bytes 4718592
  142.2 10.6 %all-to-all-start.2 = ((f32[16,1,36864]{2,1,0:T(1,128)}), f32[16,1,36864]{2,1,0:T(1,128)}, u32[]{:S(2)}, u32[]{:S(2)}) async-start(f32[16,1,36864]{2,1,0:T(1,128)} %reshape.9), calls=%async_computation.2 | async-start | bytes 4718592 | tf_op jit(solution)/shard_map/all_to_all | solution.py:19
  152.7 10.4 %copy.38 = f32[3,8,16,1536]{2,1,0,3:T(8,128)} copy(f32[3,8,16,1536]{3,2,1,0:T(8,128)S(1)} %copy-done.2) | data formatting | bytes 4718592 | tf_op jit(solution)/shard_map/all_to_all | solution.py:12
  163.2 15.9 %reshape.11 = f32[16,1,36864]{2,1,0:T(1,128)} reshape(f32[1536,3,8,16]{3,2,1,0:T(8,128)} %bitcast.57) | data formatting | bytes 4718592
  179.1 33.5 %all-to-all-done.2 = f32[16,1,36864]{2,1,0:T(1,128)} async-done(((f32[16,1,36864]{2,1,0:T(1,128)}), f32[16,1,36864]{2,1,0:T(1,128)}, u32[]{:S(2)}, u32[]{:S(2)}) %all-to-all-start.2) | async-done | bytes 2359328 | tf_op jit(solution)/shard_map/all_to_all | solution.py:19
  212.6 4.4 %all-to-all-start.3 = ((f32[16,1,36864]{2,1,0:T(1,128)}), f32[16,1,36864]{2,1,0:T(1,128)}, u32[]{:S(2)}, u32[]{:S(2)}) async-start(f32[16,1,36864]{2,1,0:T(1,128)} %reshape.11), calls=%async_computation.3 | async-start | bytes 4718592 | tf_op jit(solution)/shard_map/all_to_all | solution.py:18
  217.5 7.8 %reduce = f32[16,36864]{1,0:T(8,128)S(1)} reduce(f32[16,1,36864]{2,1,0:T(1,128)} %all-to-all-done.2, f32[]{:T(128)} %broadcast.2), dimensions={1}, to_apply=%all_to_all.60.reduce_sub_computation | reduce | bytes 4718596 | tf_op jit(solution)/shard_map/all_to_all | solution.py:19
  225.3 13.5 %reshape.10 = f32[1536,3,8,16]{3,2,1,0:T(8,128)} reshape(f32[16,36864]{1,0:T(8,128)S(1)} %reduce) | data formatting | bytes 4718592
  238.9 10.5 %copy.37 = f32[3,8,16,16,96]{4,2,1,3,0:T(8,128)S(1)} copy(f32[3,8,16,16,96]{2,1,0,4,3:T(8,128)} %bitcast.58) | data formatting | bytes 4718592 | tf_op jit(solution)/shard_map/all_to_all | solution.py:19
  251.8 20.5 %all-to-all-done.3 = f32[16,1,36864]{2,1,0:T(1,128)} async-done(((f32[16,1,36864]{2,1,0:T(1,128)}), f32[16,1,36864]{2,1,0:T(1,128)}, u32[]{:S(2)}, u32[]{:S(2)}) %all-to-all-start.3) | async-done | bytes 2359328 | tf_op jit(solution)/shard_map/all_to_all | solution.py:18
  272.3 7.8 %reduce.1 = f32[16,36864]{1,0:T(8,128)S(1)} reduce(f32[16,1,36864]{2,1,0:T(1,128)} %all-to-all-done.3, f32[]{:T(128)} %broadcast.2), dimensions={1}, to_apply=%all_to_all.64.reduce_sub_computation | reduce | bytes 4718596 | tf_op jit(solution)/shard_map/all_to_all | solution.py:18
  280.1 13.5 %reshape.12 = f32[1536,3,8,16]{3,2,1,0:T(8,128)} reshape(f32[16,36864]{1,0:T(8,128)S(1)} %reduce.1) | data formatting | bytes 4718592
  293.7 10.5 %copy.39 = f32[3,8,16,16,96]{4,2,1,3,0:T(8,128)S(1)} copy(f32[3,8,16,16,96]{2,1,0,4,3:T(8,128)} %bitcast.59) | data formatting | bytes 4718592 | tf_op jit(solution)/shard_map/all_to_all | solution.py:18
  309.5 3.8 %fusion.12 = f32[128,4608]{0,1:S(1)} fusion(f32[128,128]{1,0:T(8,128)S(1)} %copy-done.5, f32[128,4608]{0,1:T(8,128)} %bitcast.64), kind=kOutput, calls=%fused_computation.9 | convolution fusion | flops 905969664 | bytes 4784128
  (26 shorter events, 23.2 us)
Async XLA Ops:
  0.0 10.8 %copy-start = (f32[256,256]{1,0:T(8,128)S(1)}, f32[256,256]{1,0:T(8,128)}, u32[]{:S(2)}) copy-start(f32[256,256]{1,0:T(8,128)} %param.6) | copy-start | bytes 786436
  3.4 42.8 %all-to-all-start.1 = ((f32[3,8,256,96]{3,1,0,2:T(8,128)}), f32[3,8,256,96]{3,1,0,2:T(8,128)S(1)}, u32[]{:S(2)}, u32[]{:S(2)}) async-start(f32[3,8,256,96]{3,1,0,2:T(8,128)} %copy.32), calls=%async_computation.1 | async-start | bytes 6291456 | tf_op jit(solution)/shard_map/all_to_all | solution.py:12
  46.2 43.7 %all-to-all-start = ((f32[3,8,256,96]{3,1,0,2:T(8,128)}), f32[3,8,256,96]{3,1,0,2:T(8,128)}, u32[]{:S(2)}, u32[]{:S(2)}) async-start(f32[3,8,256,96]{3,1,0,2:T(8,128)} %copy.29), calls=%async_computation | async-start | bytes 6291456 | tf_op jit(solution)/shard_map/all_to_all | solution.py:13
  95.3 4.5 %copy-start.2 = (f32[3,8,16,1536]{3,2,1,0:T(8,128)S(1)}, f32[3,8,16,1536]{3,2,1,0:T(8,128)}, u32[]{:S(2)}) copy-start(f32[3,8,16,1536]{3,2,1,0:T(8,128)} %all_to_all.59) | copy-start | bytes 7077892
  95.3 4.5 %copy-start.4 = (f32[1536]{0:T(1024)S(1)}, f32[1536]{0:T(1024)}, u32[]{:S(2)}) copy-start(f32[1536]{0:T(1024)} %param.9) | copy-start | bytes 18436
  142.2 70.4 %all-to-all-start.2 = ((f32[16,1,36864]{2,1,0:T(1,128)}), f32[16,1,36864]{2,1,0:T(1,128)}, u32[]{:S(2)}, u32[]{:S(2)}) async-start(f32[16,1,36864]{2,1,0:T(1,128)} %reshape.9), calls=%async_computation.2 | async-start | bytes 4718592 | tf_op jit(solution)/shard_map/all_to_all | solution.py:19
  212.6 59.7 %all-to-all-start.3 = ((f32[16,1,36864]{2,1,0:T(1,128)}), f32[16,1,36864]{2,1,0:T(1,128)}, u32[]{:S(2)}, u32[]{:S(2)}) async-start(f32[16,1,36864]{2,1,0:T(1,128)} %reshape.11), calls=%async_computation.3 | async-start | bytes 4718592 | tf_op jit(solution)/shard_map/all_to_all | solution.py:18
  306.8 2.7 copy-start.5
  309.5 3.9 %copy-start.3 = (f32[3,128,16,96]{1,3,2,0:T(8,128)S(1)}, f32[3,128,16,96]{1,3,2,0:T(8,128)}, u32[]{:S(2)}) copy-start(f32[3,128,16,96]{1,3,2,0:T(8,128)} %copy.42) | copy-start | bytes 7077892
  313.4 2.0 copy-start.1
where the time goes:
time: 322 us; the launch traced here: 315 us
  local copies, waits for them, and re-layouts  137 us (43%)
  waiting for transfers between devices  108 us (34%)
  starting transfers between devices  28.4 us (9%)
  matrix products  24 us (7%)
  other arithmetic  17.6 us (5%)
    unnamed x17, local copies, waits for them, and re-layouts  62.4 us
    all_to_all x1, waiting for transfers between devices, per_device(): lax.all_to_all(accum, 'col', split_axis=3, concat_axis=1, tiled=True)  33.5 us
    all_to_all x1, waiting for transfers between devices, per_device(): lax.all_to_all(partial_value, 'row', split_axis=2, concat_axis=3, tiled=T...  27.2 us
    all_to_all x1, waiting for transfers between devices, per_device(): lax.all_to_all(velocity, 'row', split_axis=2, concat_axis=3, tiled=True)  26.7 us
    all_to_all x1, waiting for transfers between devices, per_device(): lax.all_to_all(fields_y, 'col', split_axis=3, concat_axis=1, tiled=True)  20.5 us
    all_to_all x4, local copies, waits for them, and re-layouts, per_device(): lax.all_to_all(velocity, 'row', split_axis=2, concat_axis=3, tiled=True)  18.9 us
    dot_general x1, matrix products, per_device(): jnp.einsum('czxy,Yy->czxY', fields_y, dy_matrix, precision=high) * metric  15 us
    all_to_all x3, local copies, waits for them, and re-layouts, per_device(): lax.all_to_all(accum, 'col', split_axis=3, concat_axis=1, tiled=True)  13.4 us
  transfers between devices with their start and end apart: 4, of which 4 were waited for; matrix products, arithmetic and copies ran while one was open for 24% of the time, Pallas kernels for 0%

commit v1 on v0

v1 whole, which is shorter than its diff:
```python
import functools

import jax
import jax.numpy as jnp
from jax import lax
from jax.experimental import pallas as pl
from jax.experimental.pallas import tpu as pltpu
from jax.sharding import PartitionSpec as P

NB, NC, YB, LN = 16, 3, 96, 128
ZB, NX, NY = 8, 256, 1536
VMEM_LIMIT = 56 * 1024 * 1024


def swap_bits(arrs, dist, shift, lane):
    low = (lane & shift) == 0
    out = list(arrs)
    for i in range(len(arrs)):
        if i & dist == 0:
            a, b = arrs[i], arrs[i | dist]
            out[i] = jnp.where(low, a, pltpu.roll(b, shift, 1))
            out[i | dist] = jnp.where(low, pltpu.roll(a, LN - shift, 1), b)
    return out


def split(v):
    high = v.astype(jnp.bfloat16)
    return high, (v - high.astype(jnp.float32)).astype(jnp.bfloat16)


def dot3(a, b, dims):
    dot = lambda x, y: lax.dot_general(x, y, (dims, ((), ())), preferred_element_type=jnp.float32)
    return dot(a[0], b[0]) + (dot(a[0], b[1]) + dot(a[1], b[0]))


def lanes8():
    return lax.broadcasted_iota(jnp.int32, (8, LN), 1)


def x_to_blocks(load, store):
    lane = lanes8()

    def body(t, _):
        rows = pl.ds(pl.multiple_of(t * 8, 8), 8)
        for half in range(2):
            arrs = [load(z, rows, half) for z in range(ZB)]
            for k in (2, 1, 0):
                arrs = swap_bits(arrs, 1 << k, 1 << k, lane)
                arrs = swap_bits(arrs, 1 << k, 16 << k, lane)
            for i in range(8):
                store(half * 8 + i, rows, arrs[i])
        return 0

    lax.fori_loop(0, YB // 8, body, 0)


def pack_kernel(v_ref, out_ref):
    def load(z, rows, half):
        return v_ref[0, z, rows, half * LN : (half + 1) * LN]

    def store(block, rows, value):
        out_ref[block, 0, rows, :] = value

    x_to_blocks(load, store)


def x_kernel(v_ref, u_ref, dx_ref, out_ref, part_ref):
    d = split(dx_ref[...])
    deriv = dot3(split(v_ref[0].reshape(ZB * YB, NX)), d, ((1,), (1,)))
    part_ref[...] = u_ref[0] * deriv.reshape(ZB, YB, NX)

    def load(z, rows, half):
        return part_ref[z, rows, half * LN : (half + 1) * LN]

    def store(block, rows, value):
        out_ref[block, 0, rows, :] = value

    x_to_blocks(load, store)


def y_kernel(v_ref, dy_ref, metric_ref, out_ref, vh_ref, vl_ref):
    step = pl.program_id(0)

    @pl.when(step == 0)
    def _():
        for c in range(NC):
            high, low = split(v_ref[:, c].reshape(NY, LN))
            vh_ref[:, c * LN : (c + 1) * LN] = high
            vl_ref[:, c * LN : (c + 1) * LN] = low

    nb = out_ref.shape[0]
    deriv = dot3(split(dy_ref[...]), (vh_ref[...], vl_ref[...]), ((1,), (0,)))
    v1 = v_ref[pl.ds(step * nb, nb), 1].reshape(nb * YB, LN) * metric_ref[...]
    for c in range(NC):
        out_ref[:, c] = (v1 * deriv[:, c * LN : (c + 1) * LN]).reshape(nb, YB, LN)


def z_to_lanes(load, store):
    lane = lanes8()

    def body(t, _):
        rows = pl.ds(pl.multiple_of(t * 8, 8), 8)
        arrs = [load(s, rows) for s in range(NB)]
        for k in range(4):
            arrs = swap_bits(arrs, 1 << k, 8 << k, lane)
        for i in range(NB):
            store((i >> 1) | ((i & 1) << 3), rows, arrs[i])
        return 0

    lax.fori_loop(0, YB // 8, body, 0)


def z_kernel(v_ref, dz_ref, out_ref, w_ref, t_ref):
    d = split(dz_ref[...])

    def gather(c, dst):
        def store(x, rows, value):
            dst[x, rows, :] = value

        z_to_lanes(lambda s, rows: v_ref[s, c, rows, :], store)

    gather(2, w_ref)
    for c in range(NC):
        src = w_ref
        if c < 2:
            gather(c, t_ref)
            src = t_ref
        deriv = dot3(split(src[...].reshape(NB * YB, LN)), d, ((1,), (1,)))
        out_ref[c] = w_ref[...] * deriv.reshape(NB, YB, LN)


def add_kernel(a_ref, w_ref, out_ref):
    def store(x, rows, value):
        out_ref[0, x, rows, :] = value + w_ref[0, x, rows, :]

    z_to_lanes(lambda s, rows: a_ref[s, 0, rows, :], store)


def call(kernel, flops=0, nbytes=0, **kw):
    return pl.pallas_call(
        kernel,
        compiler_params=pltpu.CompilerParams(vmem_limit_bytes=VMEM_LIMIT),
        cost_estimate=pl.CostEstimate(flops=flops, bytes_accessed=nbytes, transcendentals=0),
        **kw,
    )


def per_device(velocity, dx_matrix, dy_matrix, dz_matrix, metric):
    f32 = jnp.float32
    blocks = jax.ShapeDtypeStruct((NB, NC, YB, LN), f32)
    size = NB * NC * YB * LN * 4
    v = jnp.transpose(velocity, (0, 1, 3, 2))
    in_spec = pl.BlockSpec((1, ZB, YB, NX), lambda c: (c, 0, 0, 0))
    out_spec = pl.BlockSpec((NB, 1, YB, LN), lambda c: (0, c, 0, 0))
    packed = call(pack_kernel, 0, 2 * size, grid=(NC,), in_specs=[in_spec], out_specs=out_spec, out_shape=blocks)(v)
    v_y = lax.all_to_all(packed, "row", split_axis=0, concat_axis=0, tiled=True)
    part = call(
        x_kernel,
        6 * NC * ZB * YB * NX * NX,
        2 * size,
        grid=(NC,),
        in_specs=[
            in_spec,
            pl.BlockSpec((1, ZB, YB, NX), lambda c: (0, 0, 0, 0)),
            pl.BlockSpec((NX, NX), lambda c: (0, 0)),
        ],
        out_specs=out_spec,
        out_shape=blocks,
        scratch_shapes=[pltpu.VMEM((ZB, YB, NX), f32)],
    )(v, v, dx_matrix)
    part_y = lax.all_to_all(part, "row", split_axis=0, concat_axis=0, tiled=True)
    v_z = lax.all_to_all(v_y, "col", split_axis=0, concat_axis=0, tiled=True)
    yb = 4
    term_y = call(
        y_kernel,
        6 * NY * NY * NC * LN,
        2 * size + NY * NY * 4,
        grid=(NB // yb,),
        in_specs=[
            pl.BlockSpec((NB, NC, YB, LN), lambda i: (0, 0, 0, 0)),
            pl.BlockSpec((yb * YB, NY), lambda i: (i, 0)),
            pl.BlockSpec((yb * YB, LN), lambda i: (i, 0)),
        ],
        out_specs=pl.BlockSpec((yb, NC, YB, LN), lambda i: (i, 0, 0, 0)),
        out_shape=blocks,
        scratch_shapes=[pltpu.VMEM((NY, NC * LN), jnp.bfloat16)] * 2,
    )(v_y, dy_matrix, jnp.broadcast_to(metric[:, None], (NY, LN)))
    accum_z = lax.all_to_all(part_y + term_y, "col", split_axis=0, concat_axis=0, tiled=True)
    pencils = jax.ShapeDtypeStruct((NC, NB, YB, LN), f32)
    term_z = call(
        z_kernel,
        6 * NC * NB * YB * LN * LN,
        2 * size,
        grid=(1,),
        in_specs=[
            pl.BlockSpec((NB, NC, YB, LN), lambda i: (0, 0, 0, 0)),
            pl.BlockSpec((LN, LN), lambda i: (0, 0)),
        ],
        out_specs=pl.BlockSpec((NC, NB, YB, LN), lambda i: (0, 0, 0, 0)),
        out_shape=pencils,
        scratch_shapes=[pltpu.VMEM((NB, YB, LN), f32)] * 2,
    )(v_z, dz_matrix)
    pencil_spec = pl.BlockSpec((1, NB, YB, LN), lambda c: (c, 0, 0, 0))
    out = call(
        add_kernel,
        0,
        3 * size,
        grid=(NC,),
        in_specs=[out_spec, pencil_spec],
        out_specs=pencil_spec,
        out_shape=pencils,
    )(accum_z, term_z)
    return jnp.transpose(out, (0, 3, 1, 2))


def solution(mesh):
    return jax.shard_map(
        per_device,
        mesh=mesh,
        in_specs=(P(None, "col", None, "row"), P(), P(), P(), P()),
        out_specs=P(None, None, "row", "col"),
        check_vma=False,
    )
```

time: 322 us -> 235 us (0.73); the launches traced: 315 us -> 234 us
  local copies, waits for them, and re-layouts: 137 us -> 2.58 us
  Pallas kernels: 0 us -> 78.2 us
  blocking collectives: 0 us -> 34.9 us
  matrix products: 24 us -> 0 us
  other arithmetic: 17.6 us -> 3.45 us
  waiting for transfers between devices: 108 us -> 94.9 us
  starting transfers between devices: 28.4 us -> 20.4 us
    pallas_call x0 -> x5, Pallas kernels: none -> 78.2 us  [the longest x1 19.6 us: per_device(): call(x_kernel, 6 * NC * ZB * YB * NX * NX, 2 * size, grid=(NC,), in_specs...]
    unnamed x17 -> x4, local copies, waits for them, and re-layouts: 62.4 us -> 1.41 us
    all_to_all x11 -> x0, local copies, waits for them, and re-layouts: 55.3 us -> none  [the longest x4 18.9 us: per_device(): lax.all_to_all(velocity, 'row', split_axis=2, concat_axis=3, tiled=True)]
    all_to_all x0 -> x1, blocking collectives: none -> 34.9 us  [per_device(): v_y = lax.all_to_all(packed, 'row', split_axis=0, concat_axis=0, tiled=True)]
    dot_general x2 -> x0, matrix products: 20.2 us -> none  [the longest x1 15 us: per_device(): jnp.einsum('czxy,Yy->czxY', fields_y, dy_matrix, precision=high) * metric]
    all_to_all x2 -> x0, other arithmetic: 15.6 us -> none  [the longest x1 7.82 us: per_device(): lax.all_to_all(fields_y, 'col', split_axis=3, concat_axis=1, tiled=True)]
    all_to_all x4 -> x3, waiting for transfers between devices: 108 us -> 94.9 us  [the longest x1 42.5 us: per_device(): v_z = lax.all_to_all(v_y, 'col', split_axis=0, concat_axis=0, tiled=True)]
    add x1 -> x0, local copies, waits for them, and re-layouts: 11.4 us -> none  [per_device(): accum = partial_y + fields_y[1][None] * deriv_y]
  transfers between devices with their start and end apart: 4 -> 3, of which waited for: 4 -> 3; matrix products, arithmetic and copies ran while one was open for 24% -> 2% of each run, Pallas kernels for 0% -> 19%
where the time goes in v1:
time: 235 us; the launch traced here: 234 us
  waiting for transfers between devices  94.9 us (40%)
  Pallas kernels  78.2 us (33%)
  blocking collectives  34.9 us (15%)
  starting transfers between devices  20.4 us (9%)
  other arithmetic  3.45 us (1%)
  local copies, waits for them, and re-layouts  2.58 us (1%)
    all_to_all x1, waiting for transfers between devices, per_device(): v_z = lax.all_to_all(v_y, 'col', split_axis=0, concat_axis=0, tiled=True)  42.5 us
    all_to_all x1, waiting for transfers between devices, per_device(): lax.all_to_all(part_y + term_y, 'col', split_axis=0, concat_axis=0, tiled...  41.9 us
    all_to_all x1, blocking collectives, per_device(): v_y = lax.all_to_all(packed, 'row', split_axis=0, concat_axis=0, tiled=True)  34.9 us
    pallas_call x1, Pallas kernels, per_device(): call(x_kernel, 6 * NC * ZB * YB * NX * NX, 2 * size, grid=(NC,), in_specs...  19.6 us
    pallas_call x1, Pallas kernels, per_device(): call(pack_kernel, 0, 2 * size, grid=(NC,), in_specs=[in_spec], out_specs=...  17.7 us
    pallas_call x1, Pallas kernels, per_device(): call(z_kernel, 6 * NC * NB * YB * LN * LN, 2 * size, grid=(1,), in_specs=...  15.2 us
    pallas_call x1, Pallas kernels, per_device(): call(add_kernel, 0, 3 * size, grid=(NC,), in_specs=[out_spec, pencil_spec...  13.3 us
    pallas_call x1, Pallas kernels, per_device(): call(y_kernel, 6 * NY * NY * NC * LN, 2 * size + NY * NY * 4, grid=(NB //...  12.4 us
  transfers between devices with their start and end apart: 3, of which 3 were waited for; matrix products, arithmetic and copies ran while one was open for 2% of the time, Pallas kernels for 19%

profile of v1, /device:TPU:4, one launch (start us, length us, event | category | flops | bytes accessed | tf_op | source)
XLA Modules:
  0.0 234.4 jit_solution(16303107243563138333)
XLA Ops:
  0.0 19.6 %shard_map.55 = f32[16,3,96,128]{3,2,1,0:T(8,128)} custom-call(f32[3,8,96,256]{3,2,1,0:T(8,128)} %bitcast.2, f32[3,8,96,256]{3,2,1,0:T(8,128)} %bitcast.3, f32[256,256]{1,0:T(8,128)} %dx_ref.1), custom_call_target="tpu_custom_call" | custom-call | flops 905969664 | bytes 4718592 | tf_op jit(solution)/shard_map/pallas_call | solution.py:157
  19.6 6.2 %all-to-all-start = ((f32[16,3,96,128]{3,2,1,0:T(8,128)}), f32[16,3,96,128]{3,2,1,0:T(8,128)S(1)}, u32[]{:S(2)}, u32[]{:S(2)}) async-start(f32[16,3,96,128]{3,2,1,0:T(8,128)} %shard_map.55), calls=%async_computation | async-start | bytes 4718592 | tf_op jit(solution)/shard_map/all_to_all | solution.py:171
  25.8 17.7 %shard_map.56 = f32[16,3,96,128]{3,2,1,0:T(8,128)} custom-call(f32[3,8,96,256]{3,2,1,0:T(8,128)} %bitcast.4), custom_call_target="tpu_custom_call" | custom-call | bytes 4718592 | tf_op jit(solution)/shard_map/pallas_call | solution.py:155
  43.4 10.5 %all-to-all-done = f32[16,3,96,128]{3,2,1,0:T(8,128)S(1)} async-done(((f32[16,3,96,128]{3,2,1,0:T(8,128)}), f32[16,3,96,128]{3,2,1,0:T(8,128)S(1)}, u32[]{:S(2)}, u32[]{:S(2)}) %all-to-all-start) | async-done | bytes 2359328 | tf_op jit(solution)/shard_map/all_to_all | solution.py:171
  53.9 34.9 %all_to_all.20.v_ref = f32[16,3,96,128]{3,2,1,0:T(8,128)} all-to-all(f32[16,3,96,128]{3,2,1,0:T(8,128)} %shard_map.56), channel_id=1, replica_groups=mesh['row'=16,'col'=16] {'row'}, dimensions={0} | all-to-all | bytes 4718592 | tf_op jit(solution)/shard_map/all_to_all | solution.py:156
  88.8 0.0 copy-start.1
  88.8 10.5 %all-to-all-start.3 = ((f32[16,3,96,128]{3,2,1,0:T(8,128)}), f32[16,3,96,128]{3,2,1,0:T(8,128)}, u32[]{:S(2)}, u32[]{:S(2)}) async-start(f32[16,3,96,128]{3,2,1,0:T(8,128)} %all_to_all.20.v_ref), calls=%async_computation.3 | async-start | bytes 4718592 | tf_op jit(solution)/shard_map/all_to_all | solution.py:172
  99.3 0.0 copy-done.1
  99.3 1.2 broadcast_in_dim.2.metric_ref
  100.5 12.4 %shard_map.57 = f32[16,3,96,128]{3,2,1,0:T(8,128)} custom-call(f32[16,3,96,128]{3,2,1,0:T(8,128)} %all_to_all.20.v_ref, f32[1536,1536]{1,0:T(8,128)} %dy_ref.1, f32[1536,128]{1,0:T(8,128)} %broadcast_in_dim.2.metric_ref), custom_call_target="tpu_custom_call" | custom-call | flops 5435817984 | bytes 14155776 | tf_op jit(solution)/shard_map/pallas_call | solution.py:174
  112.9 3.4 %add.3 = f32[16,3,96,128]{3,2,1,0:T(8,128)} add(f32[16,3,96,128]{3,2,1,0:T(8,128)S(1)} %all-to-all-done, f32[16,3,96,128]{3,2,1,0:T(8,128)} %shard_map.57) | non-fusion elementwise | flops 589824 | bytes 7077888 | tf_op jit(solution)/shard_map/add | solution.py:188
  116.4 42.5 %all-to-all-done.3.v_ref = f32[16,3,96,128]{3,2,1,0:T(8,128)} async-done(((f32[16,3,96,128]{3,2,1,0:T(8,128)}), f32[16,3,96,128]{3,2,1,0:T(8,128)}, u32[]{:S(2)}, u32[]{:S(2)}) %all-to-all-start.3) | async-done | bytes 2359328 | tf_op jit(solution)/shard_map/all_to_all | solution.py:172
  158.9 3.7 %all-to-all-start.2 = ((f32[16,3,96,128]{3,2,1,0:T(8,128)}), f32[16,3,96,128]{3,2,1,0:T(8,128)S(1)}, u32[]{:S(2)}, u32[]{:S(2)}) async-start(f32[16,3,96,128]{3,2,1,0:T(8,128)} %add.3), calls=%async_computation.2 | async-start | bytes 4718592 | tf_op jit(solution)/shard_map/all_to_all | solution.py:188
  162.6 15.2 %shard_map.58.w_ref = f32[3,16,96,128]{3,2,1,0:T(8,128)} custom-call(f32[16,3,96,128]{3,2,1,0:T(8,128)} %all-to-all-done.3.v_ref, f32[128,128]{1,0:T(8,128)} %dz_ref.1), custom_call_target="tpu_custom_call" | custom-call | flops 452984832 | bytes 4718592 | tf_op jit(solution)/shard_map/pallas_call | solution.py:190
  177.9 41.9 %all-to-all-done.2.a_ref = f32[16,3,96,128]{3,2,1,0:T(8,128)S(1)} async-done(((f32[16,3,96,128]{3,2,1,0:T(8,128)}), f32[16,3,96,128]{3,2,1,0:T(8,128)S(1)}, u32[]{:S(2)}, u32[]{:S(2)}) %all-to-all-start.2) | async-done | bytes 2359328 | tf_op jit(solution)/shard_map/all_to_all | solution.py:188
  219.8 0.0 copy-start
  219.8 1.4 copy-done
  221.2 13.3 %shard_map.59 = f32[3,16,96,128]{3,2,1,0:T(8,128)} custom-call(f32[16,3,96,128]{3,2,1,0:T(8,128)} %copy-done, f32[3,16,96,128]{3,2,1,0:T(8,128)} %shard_map.58.w_ref), custom_call_target="tpu_custom_call" | custom-call | bytes 7077888 | tf_op jit(solution)/shard_map/pallas_call | solution.py:204
Async XLA Ops:
  19.6 34.3 %all-to-all-start = ((f32[16,3,96,128]{3,2,1,0:T(8,128)}), f32[16,3,96,128]{3,2,1,0:T(8,128)S(1)}, u32[]{:S(2)}, u32[]{:S(2)}) async-start(f32[16,3,96,128]{3,2,1,0:T(8,128)} %shard_map.55), calls=%async_computation | async-start | bytes 4718592 | tf_op jit(solution)/shard_map/all_to_all | solution.py:171
  88.8 10.5 %copy-start.1 = (f32[1536]{0:T(1024)S(1)}, f32[1536]{0:T(1024)}, u32[]{:S(2)}) copy-start(f32[1536]{0:T(1024)} %param.9) | copy-start | bytes 18436
  88.8 70.1 %all-to-all-start.3 = ((f32[16,3,96,128]{3,2,1,0:T(8,128)}), f32[16,3,96,128]{3,2,1,0:T(8,128)}, u32[]{:S(2)}, u32[]{:S(2)}) async-start(f32[16,3,96,128]{3,2,1,0:T(8,128)} %all_to_all.20.v_ref), calls=%async_computation.3 | async-start | bytes 4718592 | tf_op jit(solution)/shard_map/all_to_all | solution.py:172
  158.9 60.9 %all-to-all-start.2 = ((f32[16,3,96,128]{3,2,1,0:T(8,128)}), f32[16,3,96,128]{3,2,1,0:T(8,128)S(1)}, u32[]{:S(2)}, u32[]{:S(2)}) async-start(f32[16,3,96,128]{3,2,1,0:T(8,128)} %add.3), calls=%async_computation.2 | async-start | bytes 4718592 | tf_op jit(solution)/shard_map/all_to_all | solution.py:188
  219.8 1.4 copy-start

commit v2 on v0

v2 whole, which is shorter than its diff:
```python
import jax
import jax.numpy as jnp
from jax import lax
from jax.experimental import pallas as pl
from jax.experimental.pallas import tpu as pltpu
from jax.sharding import PartitionSpec as P

NB, NC, YB, LN = 16, 3, 96, 128
ZB, NX, NY = 8, 256, 1536
SIZE = NB * NC * YB * LN * 4
BLOCKS = jax.ShapeDtypeStruct((NB, NC, YB, LN), jnp.float32)
PENCILS = jax.ShapeDtypeStruct((NC, NB, YB, LN), jnp.float32)
VMEM = pl.BlockSpec(memory_space=pltpu.VMEM)
SMEM = pl.BlockSpec(memory_space=pltpu.SMEM)


def call(kernel, flops=0, nbytes=0, **kw):
    return pl.pallas_call(
        kernel,
        compiler_params=pltpu.CompilerParams(vmem_limit_bytes=24 * 1024 * 1024),
        cost_estimate=pl.CostEstimate(flops=flops, bytes_accessed=nbytes, transcendentals=0),
        **kw,
    )


def lanes8():
    return lax.broadcasted_iota(jnp.int32, (8, LN), 1)


def swap_bits(arrs, dist, shift, lane):
    low = (lane & shift) == 0
    out = list(arrs)
    for i in range(len(arrs)):
        if i & dist == 0:
            a, b = arrs[i], arrs[i | dist]
            out[i] = jnp.where(low, a, pltpu.roll(b, shift, 1))
            out[i | dist] = jnp.where(low, pltpu.roll(a, LN - shift, 1), b)
    return out


def zx_to_xz(a, lane):
    return jnp.take_along_axis(a, ((lane & 7) << 4) | (lane & 8) | (lane >> 4), axis=1)


def over_rows(nc, body, unroll=3):
    tiles = YB // 8

    def step(i, _):
        body(i // tiles, pl.ds(pl.multiple_of(i % tiles * 8, 8), 8))
        return 0

    lax.fori_loop(0, nc * tiles, step, 0, unroll=unroll)


def split(v):
    high = v.astype(jnp.bfloat16)
    return high, (v - high.astype(jnp.float32)).astype(jnp.bfloat16)


def dot3(a, b, dims):
    dot = lambda x, y: lax.dot_general(x, y, (dims, ((), ())), preferred_element_type=jnp.float32)
    return dot(a[0], b[0]) + (dot(a[0], b[1]) + dot(a[1], b[0]))


def x_to_blocks(load, lane, half):
    arrs = [load(z, half) for z in range(ZB)]
    for k in (2, 1, 0):
        arrs = swap_bits(arrs, 1 << k, 16 << k, lane)
    return arrs


def pack_kernel(v_ref, out_ref):
    lane = lanes8()

    def body(c, rows):
        for half in range(2):
            arrs = x_to_blocks(lambda z, h: v_ref[c, z, rows, h * LN : (h + 1) * LN], lane, half)
            for i in range(8):
                out_ref[half * 8 + i, c, rows, :] = arrs[i]

    over_rows(NC, body)


def pack(v):
    return call(pack_kernel, 0, 2 * SIZE, in_specs=[VMEM], out_specs=VMEM, out_shape=BLOCKS)(v)


def x_kernel(v_ref, dx_ref, out_ref, part_ref):
    d = split(dx_ref[...])
    for c in range(NC):
        deriv = dot3(split(v_ref[c].reshape(ZB * YB, NX)), d, ((1,), (1,)))
        part_ref[c] = v_ref[0] * deriv.reshape(ZB, YB, NX)
    lane = lanes8()

    def body(c, rows):
        for half in range(2):
            arrs = x_to_blocks(lambda z, h: part_ref[c, z, rows, h * LN : (h + 1) * LN], lane, half)
            for i in range(8):
                out_ref[half * 8 + i, c, rows, :] = zx_to_xz(arrs[i], lane)

    over_rows(NC, body)


def x_term(v, dx_matrix):
    return call(
        x_kernel,
        6 * NC * ZB * YB * NX * NX,
        2 * SIZE,
        in_specs=[VMEM, VMEM],
        out_specs=VMEM,
        out_shape=BLOCKS,
        scratch_shapes=[pltpu.VMEM((NC, ZB, YB, NX), jnp.float32)],
    )(v, dx_matrix)


def y_kernel(v_ref, dy_ref, metric_ref, out_ref, vh_ref, vl_ref, t_ref):
    step = pl.program_id(0)

    @pl.when(step == 0)
    def _():
        for c in range(NC):
            high, low = split(v_ref[:, c].reshape(NY, LN))
            vh_ref[:, c * LN : (c + 1) * LN] = high
            vl_ref[:, c * LN : (c + 1) * LN] = low

    nb = out_ref.shape[0]
    deriv = dot3(split(dy_ref[...]), (vh_ref[...], vl_ref[...]), ((1,), (0,)))
    v1 = v_ref[pl.ds(step * nb, nb), 1].reshape(nb * YB, LN) * metric_ref[...]
    for c in range(NC):
        t_ref[:, c] = (v1 * deriv[:, c * LN : (c + 1) * LN]).reshape(nb, YB, LN)
    lane = lanes8()

    def body(c, rows):
        for b in range(nb):
            out_ref[b, c, rows, :] = zx_to_xz(t_ref[b, c, rows, :], lane)

    over_rows(NC, body)


def y_term(v_y, dy_matrix, metric):
    nb = 4
    return call(
        y_kernel,
        6 * NY * NY * NC * LN,
        2 * SIZE + NY * NY * 4,
        grid=(NB // nb,),
        in_specs=[
            pl.BlockSpec((NB, NC, YB, LN), lambda i: (0, 0, 0, 0)),
            pl.BlockSpec((nb * YB, NY), lambda i: (i, 0)),
            pl.BlockSpec((nb * YB, LN), lambda i: (i, 0)),
        ],
        out_specs=pl.BlockSpec((nb, NC, YB, LN), lambda i: (i, 0, 0, 0)),
        out_shape=BLOCKS,
        scratch_shapes=[pltpu.VMEM((NY, NC * LN), jnp.bfloat16)] * 2
        + [pltpu.VMEM((nb, NC, YB, LN), jnp.float32)],
    )(v_y, dy_matrix, jnp.broadcast_to(metric[:, None], (NY, LN)))


def z_to_lanes(arrs, lane):
    for k in range(4):
        arrs = swap_bits(arrs, 1 << k, 8 << k, lane)
    return [arrs[(x & 7) * 2 + (x >> 3)] for x in range(NB)]


def z_kernel(at_ref, v_ref, dz_ref, out_ref, t_ref):
    d = split(dz_ref[...])
    lane = lanes8()
    at = [at_ref[s] for s in range(NB)]

    def body(c, rows):
        arrs = z_to_lanes([zx_to_xz(v_ref[at[s], c, rows, :], lane) for s in range(NB)], lane)
        for x in range(NB):
            t_ref[c, x, rows, :] = arrs[x]

    over_rows(NC, body)
    for c in range(NC):
        deriv = dot3(split(t_ref[c].reshape(NB * YB, LN)), d, ((1,), (1,)))
        out_ref[c] = t_ref[2] * deriv.reshape(NB, YB, LN)


def z_term(at, v_z, dz_matrix):
    return call(
        z_kernel,
        6 * NC * NB * YB * LN * LN,
        2 * SIZE,
        in_specs=[SMEM, VMEM, VMEM],
        out_specs=VMEM,
        out_shape=PENCILS,
        scratch_shapes=[pltpu.VMEM((NC, NB, YB, LN), jnp.float32)],
    )(at, v_z, dz_matrix)


def finish_kernel(a_ref, w_ref, out_ref):
    lane = lanes8()

    def body(c, rows):
        arrs = z_to_lanes([a_ref[s, c, rows, :] for s in range(NB)], lane)
        for x in range(NB):
            out_ref[c, x, rows, :] = arrs[x] + w_ref[c, x, rows, :]

    over_rows(NC, body)


def finish(accum_z, term_z):
    return call(finish_kernel, 0, 3 * SIZE, in_specs=[VMEM, VMEM], out_specs=VMEM, out_shape=PENCILS)(accum_z, term_z)


def exchange(a, axis):
    return lax.all_to_all(a, axis, split_axis=0, concat_axis=0, tiled=True)


def col_exchange(a, y, h, term):
    a = a.reshape(4, 4, NC, YB, LN)
    along_z = lambda x, s: lax.ppermute(x, "col", [(i * 4 + j, i * 4 + (j + s) % 4) for i in range(4) for j in range(4)])
    along_y = lambda x, s: lax.ppermute(x, "col", [(i * 4 + j, (i + s) % 4 * 4 + j) for i in range(4) for j in range(4)])
    take = lambda x, i, axis: lax.dynamic_index_in_dim(x, i & 3, axis, keepdims=False)
    odd = [along_z(take(a, h + s, 1), s) for s in (1, 3)]
    even = jnp.stack([take(a, h, 1), take(a, h + 2, 1)], axis=1)
    even = [take(even, y, 0)] + [along_y(take(even, y + t, 0), t) for t in (1, 2, 3)]
    two = along_z(jnp.stack([e[1] for e in even]), 2)
    odd, term = lax.optimization_barrier((odd, term))
    odd = jnp.stack(odd, axis=1)
    odd = [take(odd, y, 0)] + [along_y(take(odd, y + t, 0), t) for t in (1, 2, 3)]
    place = lambda t, s: jnp.where(s & 1, 2 * t + (s >> 1), 8 + 2 * s + t)
    at = [place((y - i) & 3, (h - j) & 3) for i in range(4) for j in range(4)]
    return term, odd, [e[0] for e in even], two, jnp.stack(at).astype(jnp.int32)


def per_device(velocity, dx_matrix, dy_matrix, dz_matrix, metric):
    me = lax.axis_index("col")
    v = jnp.transpose(velocity, (0, 1, 3, 2))
    v_y = exchange(pack(v), "row")
    part, v_y = lax.optimization_barrier((x_term(v, dx_matrix), v_y))
    term = y_term(v_y, dy_matrix, metric)
    term, odd, zero, two, at = col_exchange(v_y, me >> 2, me & 3, term)
    accum = exchange(part, "row") + term
    accum, odd, zero, two = lax.optimization_barrier((accum, odd, zero, two))
    accum_z = exchange(accum, "col")
    v_z = jnp.concatenate(odd + [jnp.stack(zero), two])
    return jnp.transpose(finish(accum_z, z_term(at, v_z, dz_matrix)), (0, 3, 1, 2))


def solution(mesh):
    return jax.shard_map(
        per_device,
        mesh=mesh,
        in_specs=(P(None, "col", None, "row"), P(), P(), P(), P()),
        out_specs=P(None, None, "row", "col"),
        check_vma=False,
    )
```

time: 322 us -> 205 us (0.64); the launches traced: 315 us -> 204 us
  local copies, waits for them, and re-layouts: 137 us -> 17.9 us
  Pallas kernels: 0 us -> 34.8 us
  matrix products: 24 us -> 0 us
  starting transfers between devices: 28.4 us -> 47.1 us
  other arithmetic: 17.6 us -> 5.34 us
  waiting for transfers between devices: 108 us -> 98.5 us
    all_to_all x11 -> x0, local copies, waits for them, and re-layouts: 55.3 us -> none  [the longest x4 18.9 us: per_device(): lax.all_to_all(velocity, 'row', split_axis=2, concat_axis=3, tiled=True)]
    unnamed x17 -> x32, local copies, waits for them, and re-layouts: 62.4 us -> 14.3 us
    all_to_all x4 -> x3, waiting for transfers between devices: 108 us -> 69.6 us  [exchange(): return lax.all_to_all(a, axis, split_axis=0, concat_axis=0, tiled=True)]
    pallas_call x0 -> x5, Pallas kernels: none -> 34.8 us  [the longest x1 14.3 us: y_term(): call(y_kernel, 6 * NY * NY * NC * LN, 2 * SIZE + NY * NY * 4, grid=(NB //...]
    ppermute x0 -> x9, waiting for transfers between devices: none -> 28.8 us  [the longest x3 15.2 us: col_exchange(): lax.ppermute(x, 'col', [(i * 4 + j, i * 4 + (j + s) % 4) for i in range(4...]
    ppermute x0 -> x9, starting transfers between devices: none -> 21.8 us  [the longest x3 11.7 us: col_exchange(): lax.ppermute(x, 'col', [(i * 4 + j, i * 4 + (j + s) % 4) for i in range(4...]
    dot_general x2 -> x0, matrix products: 20.2 us -> none  [the longest x1 15 us: per_device(): jnp.einsum('czxy,Yy->czxY', fields_y, dy_matrix, precision=high) * metric]
    all_to_all x2 -> x0, other arithmetic: 15.6 us -> none  [the longest x1 7.82 us: per_device(): lax.all_to_all(fields_y, 'col', split_axis=3, concat_axis=1, tiled=True)]
  transfers between devices with their start and end apart: 4 -> 12, of which waited for: 4 -> 8; matrix products, arithmetic and copies ran while one was open for 24% -> 6% of each run, Pallas kernels for 0% -> 13%
where the time goes in v2:
time: 205 us; the launch traced here: 204 us
  waiting for transfers between devices  98.5 us (48%)
  starting transfers between devices  47.1 us (23%)
  Pallas kernels  34.8 us (17%)
  local copies, waits for them, and re-layouts  17.9 us (9%)
  other arithmetic  5.34 us (3%)
    all_to_all x3, waiting for transfers between devices, exchange(): return lax.all_to_all(a, axis, split_axis=0, concat_axis=0, tiled=True)  69.6 us
    all_to_all x3, starting transfers between devices, exchange(): return lax.all_to_all(a, axis, split_axis=0, concat_axis=0, tiled=True)  25.3 us
    ppermute x3, waiting for transfers between devices, col_exchange(): lax.ppermute(x, 'col', [(i * 4 + j, i * 4 + (j + s) % 4) for i in range(4...  15.2 us
    unnamed x32, local copies, waits for them, and re-layouts  14.3 us
    pallas_call x1, Pallas kernels, y_term(): call(y_kernel, 6 * NY * NY * NC * LN, 2 * SIZE + NY * NY * 4, grid=(NB //...  14.3 us
    ppermute x6, waiting for transfers between devices, col_exchange(): lax.ppermute(x, 'col', [(i * 4 + j, (i + s) % 4 * 4 + j) for i in range(4...  13.7 us
    ppermute x3, starting transfers between devices, col_exchange(): lax.ppermute(x, 'col', [(i * 4 + j, i * 4 + (j + s) % 4) for i in range(4...  11.7 us
    ppermute x6, starting transfers between devices, col_exchange(): lax.ppermute(x, 'col', [(i * 4 + j, (i + s) % 4 * 4 + j) for i in range(4...  10.1 us
  transfers between devices with their start and end apart: 12, of which 8 were waited for; matrix products, arithmetic and copies ran while one was open for 6% of the time, Pallas kernels for 13%

profile of v2, /device:TPU:4, one launch (start us, length us, event | category | flops | bytes accessed | tf_op | source)
XLA Modules:
  0.0 204.0 jit_solution(10447742805342985051)
XLA Ops:
  1.7 3.2 %shard_map.56 = f32[16,3,96,128]{3,2,1,0:T(8,128)S(1)} custom-call(f32[3,8,96,256]{3,2,1,0:T(8,128)S(1)} %bitcast.57), custom_call_target="tpu_custom_call" | custom-call | bytes 4718592 | tf_op jit(solution)/shard_map/pallas_call | solution.py:85
  6.3 6.7 %all-to-all-start = ((f32[16,3,96,128]{3,2,1,0:T(8,128)}), f32[16,3,96,128]{3,2,1,0:T(8,128)}, u32[]{:S(2)}, u32[]{:S(2)}) async-start(f32[16,3,96,128]{3,2,1,0:T(8,128)} %copy-done.5), calls=%async_computation | async-start | bytes 4718592 | tf_op jit(solution)/shard_map/all_to_all | solution.py:209
  13.0 5.1 %shard_map.55 = f32[16,3,96,128]{3,2,1,0:T(8,128)S(1)} custom-call(f32[3,8,96,256]{3,2,1,0:T(8,128)S(1)} %bitcast.58, f32[256,256]{1,0:T(8,128)S(1)} %copy-done.6), custom_call_target="tpu_custom_call" | custom-call | flops 905969664 | bytes 4718592 | tf_op jit(solution)/shard_map/pallas_call | solution.py:105
  19.5 21.7 %all-to-all-done.v_ref = f32[16,3,96,128]{3,2,1,0:T(8,128)} async-done(((f32[16,3,96,128]{3,2,1,0:T(8,128)}), f32[16,3,96,128]{3,2,1,0:T(8,128)}, u32[]{:S(2)}, u32[]{:S(2)}) %all-to-all-start) | async-done | bytes 2359328 | tf_op jit(solution)/shard_map/all_to_all | solution.py:209
  41.3 6.9 %all-to-all-start.1 = ((f32[16,3,96,128]{3,2,1,0:T(8,128)}), f32[16,3,96,128]{3,2,1,0:T(8,128)}, u32[]{:S(2)}, u32[]{:S(2)}) async-start(f32[16,3,96,128]{3,2,1,0:T(8,128)} %copy-done.4), calls=%async_computation.1 | async-start | bytes 4718592 | tf_op jit(solution)/shard_map/all_to_all | solution.py:209
  48.2 1.8 constant_dynamic-slice_fusion
  50.1 2.7 %collective-permute-start.7 = (f32[2,3,96,128]{3,2,1,0:T(8,128)S(1)}, f32[2,3,96,128]{3,2,1,0:T(8,128)S(1)}, u32[]{:S(2)}, u32[]{:S(2)}) collective-permute-start(f32[2,3,96,128]{3,2,1,0:T(8,128)S(1)} %get-tuple-element.39), channel_id=1, source_target_pairs={{0,12},{1,13},{2,14},{3,15},{4,0},{5,1},{6,2},{7,3},{8,4},{9,5},{1... | collective-permute-start | bytes 884744 | tf_op jit(solution)/shard_map/ppermute | solution.py:215
  52.9 2.3 %collective-permute-start.6 = (f32[2,3,96,128]{3,2,1,0:T(8,128)S(1)}, f32[2,3,96,128]{3,2,1,0:T(8,128)S(1)}, u32[]{:S(2)}, u32[]{:S(2)}) collective-permute-start(f32[2,3,96,128]{3,2,1,0:T(8,128)S(1)} %get-tuple-element.42), channel_id=1, source_target_pairs={{0,8},{1,9},{2,10},{3,11},{4,12},{5,13},{6,14},{7,15},{8,0},{9,1},... | collective-permute-start | bytes 884744 | tf_op jit(solution)/shard_map/ppermute | solution.py:215
  55.2 5.4 %collective-permute-start.1 = (f32[4,3,96,128]{3,2,1,0:T(8,128)S(1)}, f32[4,3,96,128]{3,2,1,0:T(8,128)S(1)}, u32[]{:S(2)}, u32[]{:S(2)}) collective-permute-start(f32[4,3,96,128]{3,2,1,0:T(8,128)S(1)} %get-tuple-element.37), channel_id=1, source_target_pairs={{0,3},{1,0},{2,1},{3,2},{4,7},{5,4},{6,5},{7,6},{8,11},{9,8},{10,9... | collective-permute-start | bytes 1769480 | tf_op jit(solution)/shard_map/ppermute | solution.py:214
  60.6 5.2 %collective-permute-done.7 = f32[2,3,96,128]{3,2,1,0:T(8,128)S(1)} collective-permute-done((f32[2,3,96,128]{3,2,1,0:T(8,128)S(1)}, f32[2,3,96,128]{3,2,1,0:T(8,128)S(1)}, u32[]{:S(2)}, u32[]{:S(2)}) %collective-permute-start.7) | collective-permute-done | bytes 294944 | tf_op jit(solution)/shard_map/ppermute | solution.py:215
  65.8 3.4 %collective-permute-done.5 = f32[2,3,96,128]{3,2,1,0:T(8,128)S(1)} collective-permute-done((f32[2,3,96,128]{3,2,1,0:T(8,128)S(1)}, f32[2,3,96,128]{3,2,1,0:T(8,128)S(1)}, u32[]{:S(2)}, u32[]{:S(2)}) %collective-permute-start.5) | collective-permute-done | bytes 294944 | tf_op jit(solution)/shard_map/ppermute | solution.py:215
  71.4 6.3 %collective-permute-start.8 = (f32[4,3,96,128]{3,2,1,0:T(8,128)}, f32[4,3,96,128]{3,2,1,0:T(8,128)S(1)}, u32[]{:S(2)}, u32[]{:S(2)}) collective-permute-start(f32[4,3,96,128]{3,2,1,0:T(8,128)} %pad_maximum_fusion), channel_id=1, source_target_pairs={{0,2},{1,3},{2,0},{3,1},{4,6},{5,7},{6,4},{7,5},{8,10},{9,11},{10,... | collective-permute-start | bytes 1769480 | tf_op jit(solution)/shard_map/ppermute | solution.py:214
  78.0 3.7 %copy-done.8 = f32[1536,1536]{1,0:T(8,128)S(1)} copy-done((f32[1536,1536]{1,0:T(8,128)S(1)}, f32[1536,1536]{1,0:T(8,128)}, u32[]{:S(2)}) %copy-start.8) | copy-done | bytes 9437208
  81.6 14.3 %shard_map.57 = f32[16,3,96,128]{3,2,1,0:T(8,128)S(1)} custom-call(f32[16,3,96,128]{3,2,1,0:T(8,128)} %all-to-all-done.v_ref, f32[1536,1536]{1,0:T(8,128)S(1)} %copy-done.8, f32[1536,128]{1,0:T(8,128)S(1)} %broadcast_in_dim.2.metric_ref), custom_call_target="tpu_custom_call" | custom-call | flops 5435817984 | bytes 14155776 | tf_op jit(solution)/shard_map/pallas_call | solution.py:142
  96.0 10.3 %collective-permute-done = f32[4,3,96,128]{3,2,1,0:T(8,128)S(1)} collective-permute-done((f32[4,3,96,128]{3,2,1,0:T(8,128)S(1)}, f32[4,3,96,128]{3,2,1,0:T(8,128)S(1)}, u32[]{:S(2)}, u32[]{:S(2)}) %collective-permute-start) | collective-permute-done | bytes 589856 | tf_op jit(solution)/shard_map/ppermute | solution.py:214
  107.2 2.9 %collective-permute-start.4 = (f32[2,3,96,128]{3,2,1,0:T(8,128)}, f32[2,3,96,128]{3,2,1,0:T(8,128)}, u32[]{:S(2)}, u32[]{:S(2)}) collective-permute-start(f32[2,3,96,128]{3,2,1,0:T(8,128)} %get-tuple-element.43), channel_id=1, source_target_pairs={{0,12},{1,13},{2,14},{3,15},{4,0},{5,1},{6,2},{7,3},{8,4},{9,5},{1... | collective-permute-start | bytes 884744 | tf_op jit(solution)/shard_map/ppermute | solution.py:215
  110.1 2.2 %collective-permute-start.3 = (f32[2,3,96,128]{3,2,1,0:T(8,128)}, f32[2,3,96,128]{3,2,1,0:T(8,128)}, u32[]{:S(2)}, u32[]{:S(2)}) collective-permute-start(f32[2,3,96,128]{3,2,1,0:T(8,128)} %get-tuple-element.46), channel_id=1, source_target_pairs={{0,8},{1,9},{2,10},{3,11},{4,12},{5,13},{6,14},{7,15},{8,0},{9,1},... | collective-permute-start | bytes 884744 | tf_op jit(solution)/shard_map/ppermute | solution.py:215
  112.3 3.4 %add.184 = f32[16,3,96,128]{3,2,1,0:T(8,128)} add(f32[16,3,96,128]{3,2,1,0:T(8,128)} %all-to-all-done.1, f32[16,3,96,128]{3,2,1,0:T(8,128)S(1)} %shard_map.57) | non-fusion elementwise | flops 589824 | bytes 7077888 | tf_op jit(solution)/shard_map/add | solution.py:236
  115.8 4.8 %collective-permute-done.8 = f32[4,3,96,128]{3,2,1,0:T(8,128)S(1)} collective-permute-done((f32[4,3,96,128]{3,2,1,0:T(8,128)}, f32[4,3,96,128]{3,2,1,0:T(8,128)S(1)}, u32[]{:S(2)}, u32[]{:S(2)}) %collective-permute-start.8) | collective-permute-done | bytes 589856 | tf_op jit(solution)/shard_map/ppermute | solution.py:214
  122.3 3.4 %collective-permute-done.2 = f32[2,3,96,128]{3,2,1,0:T(8,128)} collective-permute-done((f32[2,3,96,128]{3,2,1,0:T(8,128)}, f32[2,3,96,128]{3,2,1,0:T(8,128)}, u32[]{:S(2)}, u32[]{:S(2)}) %collective-permute-start.2) | collective-permute-done | bytes 294944 | tf_op jit(solution)/shard_map/ppermute | solution.py:215
  125.7 11.6 %all-to-all-start.2 = ((f32[16,3,96,128]{3,2,1,0:T(8,128)}), f32[16,3,96,128]{3,2,1,0:T(8,128)S(1)}, u32[]{:S(2)}, u32[]{:S(2)}) async-start(f32[16,3,96,128]{3,2,1,0:T(8,128)} %add.184), calls=%async_computation.2 | async-start | bytes 4718592 | tf_op jit(solution)/shard_map/all_to_all | solution.py:209
  140.8 6.7 %shard_map.58.w_ref = f32[3,16,96,128]{3,2,1,0:T(8,128)S(1)} custom-call(s32[16]{0:T(128)S(1)} %stack.101.at_ref, f32[16,3,96,128]{3,2,1,0:T(8,128)S(1)} %constant_dynamic-update-slice_fusion.v_ref, f32[128,128]{1,0:T(8,128)S(1)} %copy-done.7), custom_call_target="tpu_custom_call" | custom-call | flops 452984832 | bytes 4718592 | tf_op jit(solution)/shard_map/pallas_call | solution.py:182
  148.9 47.9 %all-to-all-done.2.a_ref = f32[16,3,96,128]{3,2,1,0:T(8,128)S(1)} async-done(((f32[16,3,96,128]{3,2,1,0:T(8,128)}), f32[16,3,96,128]{3,2,1,0:T(8,128)S(1)}, u32[]{:S(2)}, u32[]{:S(2)}) %all-to-all-start.2) | async-done | bytes 2359328 | tf_op jit(solution)/shard_map/all_to_all | solution.py:209
  198.4 5.5 %shard_map.59 = f32[3,16,96,128]{3,2,1,0:T(8,128)} custom-call(f32[16,3,96,128]{3,2,1,0:T(8,128)S(1)} %all-to-all-done.2.a_ref, f32[3,16,96,128]{3,2,1,0:T(8,128)S(1)} %copy-done.1), custom_call_target="tpu_custom_call" | custom-call | bytes 7077888 | tf_op jit(solution)/shard_map/pallas_call | solution.py:205
  (49 shorter events, 16.1 us)
Async XLA Ops:
  0.0 1.7 copy-start.2
  4.9 1.4 copy-start.5
  6.3 6.7 %copy-start.3 = (f32[3,8,256,96]{2,3,1,0:T(8,128)S(1)}, f32[3,8,256,96]{2,3,1,0:T(8,128)}, u32[]{:S(2)}) copy-start(f32[3,8,256,96]{2,3,1,0:T(8,128)} %param.5) | copy-start | bytes 7077892
  6.3 6.8 %copy-start.6 = (f32[256,256]{1,0:T(8,128)S(1)}, f32[256,256]{1,0:T(8,128)}, u32[]{:S(2)}) copy-start(f32[256,256]{1,0:T(8,128)} %dx_ref.1) | copy-start | bytes 786436
  6.3 35.0 %all-to-all-start = ((f32[16,3,96,128]{3,2,1,0:T(8,128)}), f32[16,3,96,128]{3,2,1,0:T(8,128)}, u32[]{:S(2)}, u32[]{:S(2)}) async-start(f32[16,3,96,128]{3,2,1,0:T(8,128)} %copy-done.5), calls=%async_computation | async-start | bytes 4718592 | tf_op jit(solution)/shard_map/all_to_all | solution.py:209
  18.1 1.4 copy-start.4
  41.3 71.1 %all-to-all-start.1 = ((f32[16,3,96,128]{3,2,1,0:T(8,128)}), f32[16,3,96,128]{3,2,1,0:T(8,128)}, u32[]{:S(2)}, u32[]{:S(2)}) async-start(f32[16,3,96,128]{3,2,1,0:T(8,128)} %copy-done.4), calls=%async_computation.1 | async-start | bytes 4718592 | tf_op jit(solution)/shard_map/all_to_all | solution.py:209
  50.1 27.6 %copy-start.11 = (f32[1536]{0:T(1024)S(1)}, f32[1536]{0:T(1024)}, u32[]{:S(2)}) copy-start(f32[1536]{0:T(1024)} %param.9) | copy-start | bytes 18436
  50.1 15.7 %collective-permute-start.7 = (f32[2,3,96,128]{3,2,1,0:T(8,128)S(1)}, f32[2,3,96,128]{3,2,1,0:T(8,128)S(1)}, u32[]{:S(2)}, u32[]{:S(2)}) collective-permute-start(f32[2,3,96,128]{3,2,1,0:T(8,128)S(1)} %get-tuple-element.39), channel_id=1, source_target_pairs={{0,12},{1,13},{2,14},{3,15},{4,0},{5,1},{6,2},{7,3},{8,4},{9,5},{1... | collective-permute-start | bytes 884744 | tf_op jit(solution)/shard_map/ppermute | solution.py:215
  52.8 16.3 %collective-permute-start.5 = (f32[2,3,96,128]{3,2,1,0:T(8,128)S(1)}, f32[2,3,96,128]{3,2,1,0:T(8,128)S(1)}, u32[]{:S(2)}, u32[]{:S(2)}) collective-permute-start(f32[2,3,96,128]{3,2,1,0:T(8,128)S(1)} %get-tuple-element.41), channel_id=1, source_target_pairs={{0,4},{1,5},{2,6},{3,7},{4,8},{5,9},{6,10},{7,11},{8,12},{9,13},{1... | collective-permute-start | bytes 884744 | tf_op jit(solution)/shard_map/ppermute | solution.py:215
  52.9 17.0 %collective-permute-start.6 = (f32[2,3,96,128]{3,2,1,0:T(8,128)S(1)}, f32[2,3,96,128]{3,2,1,0:T(8,128)S(1)}, u32[]{:S(2)}, u32[]{:S(2)}) collective-permute-start(f32[2,3,96,128]{3,2,1,0:T(8,128)S(1)} %get-tuple-element.42), channel_id=1, source_target_pairs={{0,8},{1,9},{2,10},{3,11},{4,12},{5,13},{6,14},{7,15},{8,0},{9,1},... | collective-permute-start | bytes 884744 | tf_op jit(solution)/shard_map/ppermute | solution.py:215
  55.2 40.8 %collective-permute-start.1 = (f32[4,3,96,128]{3,2,1,0:T(8,128)S(1)}, f32[4,3,96,128]{3,2,1,0:T(8,128)S(1)}, u32[]{:S(2)}, u32[]{:S(2)}) collective-permute-start(f32[4,3,96,128]{3,2,1,0:T(8,128)S(1)} %get-tuple-element.37), channel_id=1, source_target_pairs={{0,3},{1,0},{2,1},{3,2},{4,7},{5,4},{6,5},{7,6},{8,11},{9,8},{10,9... | collective-permute-start | bytes 1769480 | tf_op jit(solution)/shard_map/ppermute | solution.py:214
  60.6 45.7 %collective-permute-start = (f32[4,3,96,128]{3,2,1,0:T(8,128)S(1)}, f32[4,3,96,128]{3,2,1,0:T(8,128)S(1)}, u32[]{:S(2)}, u32[]{:S(2)}) collective-permute-start(f32[4,3,96,128]{3,2,1,0:T(8,128)S(1)} %get-tuple-element.38), channel_id=1, source_target_pairs={{0,1},{1,2},{2,3},{3,0},{4,5},{5,6},{6,7},{7,4},{8,9},{9,10},{10,1... | collective-permute-start | bytes 1769480 | tf_op jit(solution)/shard_map/ppermute | solution.py:214
  71.4 49.2 %collective-permute-start.8 = (f32[4,3,96,128]{3,2,1,0:T(8,128)}, f32[4,3,96,128]{3,2,1,0:T(8,128)S(1)}, u32[]{:S(2)}, u32[]{:S(2)}) collective-permute-start(f32[4,3,96,128]{3,2,1,0:T(8,128)} %pad_maximum_fusion), channel_id=1, source_target_pairs={{0,2},{1,3},{2,0},{3,1},{4,6},{5,7},{6,4},{7,5},{8,10},{9,11},{10,... | collective-permute-start | bytes 1769480 | tf_op jit(solution)/shard_map/ppermute | solution.py:214
  77.9 3.7 %copy-start.8 = (f32[1536,1536]{1,0:T(8,128)S(1)}, f32[1536,1536]{1,0:T(8,128)}, u32[]{:S(2)}) copy-start(f32[1536,1536]{1,0:T(8,128)} %dy_ref.1) | copy-start | bytes 28311556
  107.2 15.1 %collective-permute-start.4 = (f32[2,3,96,128]{3,2,1,0:T(8,128)}, f32[2,3,96,128]{3,2,1,0:T(8,128)}, u32[]{:S(2)}, u32[]{:S(2)}) collective-permute-start(f32[2,3,96,128]{3,2,1,0:T(8,128)} %get-tuple-element.43), channel_id=1, source_target_pairs={{0,12},{1,13},{2,14},{3,15},{4,0},{5,1},{6,2},{7,3},{8,4},{9,5},{1... | collective-permute-start | bytes 884744 | tf_op jit(solution)/shard_map/ppermute | solution.py:215
  110.1 15.6 %collective-permute-start.2 = (f32[2,3,96,128]{3,2,1,0:T(8,128)}, f32[2,3,96,128]{3,2,1,0:T(8,128)}, u32[]{:S(2)}, u32[]{:S(2)}) collective-permute-start(f32[2,3,96,128]{3,2,1,0:T(8,128)} %get-tuple-element.45), channel_id=1, source_target_pairs={{0,4},{1,5},{2,6},{3,7},{4,8},{5,9},{6,10},{7,11},{8,12},{9,13},{1... | collective-permute-start | bytes 884744 | tf_op jit(solution)/shard_map/ppermute | solution.py:215
  110.1 15.6 %collective-permute-start.3 = (f32[2,3,96,128]{3,2,1,0:T(8,128)}, f32[2,3,96,128]{3,2,1,0:T(8,128)}, u32[]{:S(2)}, u32[]{:S(2)}) collective-permute-start(f32[2,3,96,128]{3,2,1,0:T(8,128)} %get-tuple-element.46), channel_id=1, source_target_pairs={{0,8},{1,9},{2,10},{3,11},{4,12},{5,13},{6,14},{7,15},{8,0},{9,1},... | collective-permute-start | bytes 884744 | tf_op jit(solution)/shard_map/ppermute | solution.py:215
  125.7 71.0 %all-to-all-start.2 = ((f32[16,3,96,128]{3,2,1,0:T(8,128)}), f32[16,3,96,128]{3,2,1,0:T(8,128)S(1)}, u32[]{:S(2)}, u32[]{:S(2)}) async-start(f32[16,3,96,128]{3,2,1,0:T(8,128)} %add.184), calls=%async_computation.2 | async-start | bytes 4718592 | tf_op jit(solution)/shard_map/all_to_all | solution.py:209
  137.5 3.1 %copy-start.9 = (f32[3,96,128]{2,1,0:T(8,128)S(1)}, f32[3,96,128]{2,1,0:T(8,128)}, u32[]{:S(2)}) copy-start(f32[3,96,128]{2,1,0:T(8,128)} %get-tuple-element.31) | copy-start | bytes 442372
  137.5 3.1 %copy-start.10 = (f32[3,96,128]{2,1,0:T(8,128)S(1)}, f32[3,96,128]{2,1,0:T(8,128)}, u32[]{:S(2)}) copy-start(f32[3,96,128]{2,1,0:T(8,128)} %get-tuple-element.32) | copy-start | bytes 442372
  137.5 3.2 %copy-start.7 = (f32[128,128]{1,0:T(8,128)S(1)}, f32[128,128]{1,0:T(8,128)}, u32[]{:S(2)}) copy-start(f32[128,128]{1,0:T(8,128)} %dz_ref.1) | copy-start | bytes 196612
  147.4 1.4 copy-start
  196.8 1.7 copy-start.1

commit v3 on v2

--- a/solution.py
+++ b/solution.py
@@ -12,12 +12,13 @@
 PENCILS = jax.ShapeDtypeStruct((NC, NB, YB, LN), jnp.float32)
 VMEM = pl.BlockSpec(memory_space=pltpu.VMEM)
 SMEM = pl.BlockSpec(memory_space=pltpu.SMEM)
-
-
-def call(kernel, flops=0, nbytes=0, **kw):
+HBM = pl.BlockSpec(memory_space=pltpu.HBM)
+
+
+def call(kernel, flops=0, nbytes=0, limit=24, **kw):
     return pl.pallas_call(
         kernel,
-        compiler_params=pltpu.CompilerParams(vmem_limit_bytes=24 * 1024 * 1024),
+        compiler_params=pltpu.CompilerParams(vmem_limit_bytes=limit * 1024 * 1024),
         cost_estimate=pl.CostEstimate(flops=flops, bytes_accessed=nbytes, transcendentals=0),
         **kw,
     )
@@ -38,18 +39,22 @@
     return out
 
 
-def zx_to_xz(a, lane):
-    return jnp.take_along_axis(a, ((lane & 7) << 4) | (lane & 8) | (lane >> 4), axis=1)
-
-
-def over_rows(nc, body, unroll=3):
+def zx_to_xz(lane, block):
+    lane = (lane - 8 * block) & (LN - 1)
+    return ((lane & 7) << 4) | (lane & 8) | (lane >> 4)
+
+
+def over_rows(components, body):
     tiles = YB // 8
 
     def step(i, _):
-        body(i // tiles, pl.ds(pl.multiple_of(i % tiles * 8, 8), 8))
+        body(components[0] + i // tiles, pl.ds(pl.multiple_of(i % tiles * 8, 8), 8))
         return 0
 
-    lax.fori_loop(0, nc * tiles, step, 0, unroll=unroll)
+    lax.fori_loop(0, len(components) * tiles, step, 0, unroll=3)
+
+
+ALL = range(NC)
 
 
 def split(v):
@@ -69,51 +74,74 @@
     return arrs
 
 
-def pack_kernel(v_ref, out_ref):
+def pack_kernel(v_hbm, out_hbm, v_ref, out_ref, sems):
     lane = lanes8()
+    loads = [pltpu.make_async_copy(v_hbm.at[c], v_ref.at[c], sems.at[c]) for c in ALL]
+    stores = [pltpu.make_async_copy(out_ref.at[c], out_hbm.at[:, c], sems.at[NC + c]) for c in ALL]
+    for load in loads:
+        load.start()
 
     def body(c, rows):
         for half in range(2):
             arrs = x_to_blocks(lambda z, h: v_ref[c, z, rows, h * LN : (h + 1) * LN], lane, half)
             for i in range(8):
-                out_ref[half * 8 + i, c, rows, :] = arrs[i]
-
-    over_rows(NC, body)
+                out_ref[c, half * 8 + i, rows, :] = arrs[i]
+
+    for c in ALL:
+        loads[c].wait()
+        over_rows([c], body)
+        stores[c].start()
+    for store in stores:
+        store.wait()
 
 
 def pack(v):
-    return call(pack_kernel, 0, 2 * SIZE, in_specs=[VMEM], out_specs=VMEM, out_shape=BLOCKS)(v)
-
-
-def x_kernel(v_ref, dx_ref, out_ref, part_ref):
+    return call(
+        pack_kernel,
+        0,
+        2 * SIZE,
+        limit=56,
+        in_specs=[HBM],
+        out_specs=HBM,
+        out_shape=BLOCKS,
+        scratch_shapes=[
+            pltpu.VMEM((NC, ZB, YB, NX), jnp.float32),
+            pltpu.VMEM((NC, NB, YB, LN), jnp.float32),
+            pltpu.SemaphoreType.DMA((2 * NC,)),
+        ],
+    )(v)
+
+
+def x_kernel(block_ref, v_ref, dx_ref, out_ref, part_ref):
     d = split(dx_ref[...])
     for c in range(NC):
         deriv = dot3(split(v_ref[c].reshape(ZB * YB, NX)), d, ((1,), (1,)))
         part_ref[c] = v_ref[0] * deriv.reshape(ZB, YB, NX)
     lane = lanes8()
+    order = zx_to_xz(lane, block_ref[0])
 
     def body(c, rows):
         for half in range(2):
             arrs = x_to_blocks(lambda z, h: part_ref[c, z, rows, h * LN : (h + 1) * LN], lane, half)
             for i in range(8):
-                out_ref[half * 8 + i, c, rows, :] = zx_to_xz(arrs[i], lane)
-
-    over_rows(NC, body)
-
-
-def x_term(v, dx_matrix):
+                out_ref[half * 8 + i, c, rows, :] = jnp.take_along_axis(arrs[i], order, axis=1)
+
+    over_rows(ALL, body)
+
+
+def x_term(block, v, dx_matrix):
     return call(
         x_kernel,
         6 * NC * ZB * YB * NX * NX,
         2 * SIZE,
-        in_specs=[VMEM, VMEM],
+        in_specs=[SMEM, VMEM, VMEM],
         out_specs=VMEM,
         out_shape=BLOCKS,
         scratch_shapes=[pltpu.VMEM((NC, ZB, YB, NX), jnp.float32)],
-    )(v, dx_matrix)
-
-
-def y_kernel(v_ref, dy_ref, metric_ref, out_ref, vh_ref, vl_ref, t_ref):
+    )(block, v, dx_matrix)
+
+
+def y_kernel(block_ref, v_ref, dy_ref, metric_ref, out_ref, vh_ref, vl_ref, t_ref):
     step = pl.program_id(0)
 
     @pl.when(step == 0)
@@ -128,16 +156,16 @@
     v1 = v_ref[pl.ds(step * nb, nb), 1].reshape(nb * YB, LN) * metric_ref[...]
     for c in range(NC):
         t_ref[:, c] = (v1 * deriv[:, c * LN : (c + 1) * LN]).reshape(nb, YB, LN)
-    lane = lanes8()
+    order = zx_to_xz(lanes8(), block_ref[0])
 
     def body(c, rows):
         for b in range(nb):
-            out_ref[b, c, rows, :] = zx_to_xz(t_ref[b, c, rows, :], lane)
-
-    over_rows(NC, body)
-
-
-def y_term(v_y, dy_matrix, metric):
+            out_ref[b, c, rows, :] = jnp.take_along_axis(t_ref[b, c, rows, :], order, axis=1)
+
+    over_rows(ALL, body)
+
+
+def y_term(block, v_y, dy_matrix, metric):
     nb = 4
     return call(
         y_kernel,
@@ -145,6 +173,7 @@
         2 * SIZE + NY * NY * 4,
         grid=(NB // nb,),
         in_specs=[
+            SMEM,
             pl.BlockSpec((NB, NC, YB, LN), lambda i: (0, 0, 0, 0)),
             pl.BlockSpec((nb * YB, NY), lambda i: (i, 0)),
             pl.BlockSpec((nb * YB, LN), lambda i: (i, 0)),
@@ -153,13 +182,15 @@
         out_shape=BLOCKS,
         scratch_shapes=[pltpu.VMEM((NY, NC * LN), jnp.bfloat16)] * 2
         + [pltpu.VMEM((nb, NC, YB, LN), jnp.float32)],
-    )(v_y, dy_matrix, jnp.broadcast_to(metric[:, None], (NY, LN)))
+    )(block, v_y, dy_matrix, jnp.broadcast_to(metric[:, None], (NY, LN)))
 
 
 def z_to_lanes(arrs, lane):
     for k in range(4):
-        arrs = swap_bits(arrs, 1 << k, 8 << k, lane)
-    return [arrs[(x & 7) * 2 + (x >> 3)] for x in range(NB)]
+        high = (lane & 8 << k) != 0
+        arrs = [jnp.where(high, arrs[(i + (1 << k)) % NB], arrs[i]) for i in range(NB)]
+    turned = [pltpu.roll(arrs[-g % NB], (LN - 8 * g) % LN, 1) if g else arrs[0] for g in range(NB)]
+    return [turned[(x & 7) * 2 + (x >> 3)] for x in range(NB)]
 
 
 def z_kernel(at_ref, v_ref, dz_ref, out_ref, t_ref):
@@ -168,11 +199,12 @@
     at = [at_ref[s] for s in range(NB)]
 
     def body(c, rows):
-        arrs = z_to_lanes([zx_to_xz(v_ref[at[s], c, rows, :], lane) for s in range(NB)], lane)
+        arrs = [jnp.take_along_axis(v_ref[at[s], c, rows, :], zx_to_xz(lane, s), axis=1) for s in range(NB)]
+        arrs = z_to_lanes(arrs, lane)
         for x in range(NB):
             t_ref[c, x, rows, :] = arrs[x]
 
-    over_rows(NC, body)
+    over_rows(ALL, body)
     for c in range(NC):
         deriv = dot3(split(t_ref[c].reshape(NB * YB, LN)), d, ((1,), (1,)))
         out_ref[c] = t_ref[2] * deriv.reshape(NB, YB, LN)
@@ -190,19 +222,36 @@
     )(at, v_z, dz_matrix)
 
 
-def finish_kernel(a_ref, w_ref, out_ref):
+def finish_kernel(a_ref, w_hbm, out_hbm, w_ref, sems):
     lane = lanes8()
+    loads = [pltpu.make_async_copy(w_hbm.at[c], w_ref.at[c], sems.at[c]) for c in ALL]
+    stores = [pltpu.make_async_copy(w_ref.at[c], out_hbm.at[c], sems.at[NC + c]) for c in ALL]
+    for load in loads:
+        load.start()
 
     def body(c, rows):
         arrs = z_to_lanes([a_ref[s, c, rows, :] for s in range(NB)], lane)
         for x in range(NB):
-            out_ref[c, x, rows, :] = arrs[x] + w_ref[c, x, rows, :]
-
-    over_rows(NC, body)
+            w_ref[c, x, rows, :] += arrs[x]
+
+    for c in ALL:
+        loads[c].wait()
+        over_rows([c], body)
+        stores[c].start()
+    for store in stores:
+        store.wait()
 
 
 def finish(accum_z, term_z):
-    return call(finish_kernel, 0, 3 * SIZE, in_specs=[VMEM, VMEM], out_specs=VMEM, out_shape=PENCILS)(accum_z, term_z)
+    return call(
+        finish_kernel,
+        0,
+        3 * SIZE,
+        in_specs=[VMEM, HBM],
+        out_specs=HBM,
+        out_shape=PENCILS,
+        scratch_shapes=[pltpu.VMEM(PENCILS.shape, jnp.float32), pltpu.SemaphoreType.DMA((2 * NC,))],
+    )(accum_z, term_z)
 
 
 def exchange(a, axis):
@@ -228,10 +277,11 @@
 
 def per_device(velocity, dx_matrix, dy_matrix, dz_matrix, metric):
     me = lax.axis_index("col")
+    block = me.reshape(1).astype(jnp.int32)
     v = jnp.transpose(velocity, (0, 1, 3, 2))
     v_y = exchange(pack(v), "row")
-    part, v_y = lax.optimization_barrier((x_term(v, dx_matrix), v_y))
-    term = y_term(v_y, dy_matrix, metric)
+    part, v_y = lax.optimization_barrier((x_term(block, v, dx_matrix), v_y))
+    term = y_term(block, v_y, dy_matrix, metric)
     term, odd, zero, two, at = col_exchange(v_y, me >> 2, me & 3, term)
     accum = exchange(part, "row") + term
     accum, odd, zero, two = lax.optimization_barrier((accum, odd, zero, two))

time: 205 us -> 201 us (0.980)
  local copies, waits for them, and re-layouts: 17.9 us -> 14.8 us
  Pallas kernels: 34.8 us -> 32.4 us
    unnamed x32 -> x28, local copies, waits for them, and re-layouts: 14.3 us -> 11.3 us
  transfers between devices with their start and end apart: 12 -> 12, of which waited for: 8 -> 8; matrix products, arithmetic and copies ran while one was open for 6% -> 6% of each run, Pallas kernels for 13% -> 12%
where the time goes in v3:
time: 201 us; the launch traced here: 200 us
  waiting for transfers between devices  100 us (50%)
  starting transfers between devices  47 us (23%)
  Pallas kernels  32.4 us (16%)
  local copies, waits for them, and re-layouts  14.8 us (7%)
  other arithmetic  5.33 us (3%)
    all_to_all x3, waiting for transfers between devices, exchange(): return lax.all_to_all(a, axis, split_axis=0, concat_axis=0, tiled=True)  71.2 us
    all_to_all x3, starting transfers between devices, exchange(): return lax.all_to_all(a, axis, split_axis=0, concat_axis=0, tiled=True)  25.2 us
    ppermute x3, waiting for transfers between devices, col_exchange(): lax.ppermute(x, 'col', [(i * 4 + j, i * 4 + (j + s) % 4) for i in range(4...  15.3 us
    pallas_call x1, Pallas kernels, y_term(): call(y_kernel, 6 * NY * NY * NC * LN, 2 * SIZE + NY * NY * 4, grid=(NB //...  14.2 us
    ppermute x6, waiting for transfers between devices, col_exchange(): lax.ppermute(x, 'col', [(i * 4 + j, (i + s) % 4 * 4 + j) for i in range(4...  13.7 us
    ppermute x3, starting transfers between devices, col_exchange(): lax.ppermute(x, 'col', [(i * 4 + j, i * 4 + (j + s) % 4) for i in range(4...  11.7 us
    unnamed x28, local copies, waits for them, and re-layouts  11.3 us
    ppermute x6, starting transfers between devices, col_exchange(): lax.ppermute(x, 'col', [(i * 4 + j, (i + s) % 4 * 4 + j) for i in range(4...  10.2 us
  transfers between devices with their start and end apart: 12, of which 8 were waited for; matrix products, arithmetic and copies ran while one was open for 6% of the time, Pallas kernels for 12%

profile of v3, /device:TPU:4, one launch (start us, length us, event | category | flops | bytes accessed | tf_op | source)
XLA Modules:
  0.0 200.1 jit_solution(12473281801839821819)
XLA Ops:
  0.0 5.3 %shard_map.56 = f32[16,3,96,128]{3,2,1,0:T(8,128)} custom-call(f32[3,8,96,256]{3,2,1,0:T(8,128)} %bitcast.58), custom_call_target="tpu_custom_call" | custom-call | bytes 4718592 | tf_op jit(solution)/shard_map/pallas_call | solution.py:99
  5.3 6.6 %all-to-all-start = ((f32[16,3,96,128]{3,2,1,0:T(8,128)}), f32[16,3,96,128]{3,2,1,0:T(8,128)}, u32[]{:S(2)}, u32[]{:S(2)}) async-start(f32[16,3,96,128]{3,2,1,0:T(8,128)} %shard_map.56), calls=%async_computation | async-start | bytes 4718592 | tf_op jit(solution)/shard_map/all_to_all | solution.py:258
  11.9 5.1 %shard_map.55 = f32[16,3,96,128]{3,2,1,0:T(8,128)S(1)} custom-call(s32[1]{0:T(128)} %bitcast.block_ref, f32[3,8,96,256]{3,2,1,0:T(8,128)S(1)} %bitcast.59, f32[256,256]{1,0:T(8,128)S(1)} %copy-done.4), custom_call_target="tpu_custom_call" | custom-call | flops 905969664 | bytes 4718592 | tf_op jit(solution)/shard_map/pallas_call | solution.py:133
  18.5 21.7 %all-to-all-done.v_ref = f32[16,3,96,128]{3,2,1,0:T(8,128)} async-done(((f32[16,3,96,128]{3,2,1,0:T(8,128)}), f32[16,3,96,128]{3,2,1,0:T(8,128)}, u32[]{:S(2)}, u32[]{:S(2)}) %all-to-all-start) | async-done | bytes 2359328 | tf_op jit(solution)/shard_map/all_to_all | solution.py:258
  40.2 6.9 %all-to-all-start.1 = ((f32[16,3,96,128]{3,2,1,0:T(8,128)}), f32[16,3,96,128]{3,2,1,0:T(8,128)}, u32[]{:S(2)}, u32[]{:S(2)}) async-start(f32[16,3,96,128]{3,2,1,0:T(8,128)} %copy-done.3), calls=%async_computation.1 | async-start | bytes 4718592 | tf_op jit(solution)/shard_map/all_to_all | solution.py:258
  47.1 1.8 constant_dynamic-slice_fusion
  49.0 2.7 %collective-permute-start.7 = (f32[2,3,96,128]{3,2,1,0:T(8,128)S(1)}, f32[2,3,96,128]{3,2,1,0:T(8,128)S(1)}, u32[]{:S(2)}, u32[]{:S(2)}) collective-permute-start(f32[2,3,96,128]{3,2,1,0:T(8,128)S(1)} %get-tuple-element.39), channel_id=1, source_target_pairs={{0,12},{1,13},{2,14},{3,15},{4,0},{5,1},{6,2},{7,3},{8,4},{9,5},{1... | collective-permute-start | bytes 884744 | tf_op jit(solution)/shard_map/ppermute | solution.py:264
  51.8 2.3 %collective-permute-start.6 = (f32[2,3,96,128]{3,2,1,0:T(8,128)S(1)}, f32[2,3,96,128]{3,2,1,0:T(8,128)S(1)}, u32[]{:S(2)}, u32[]{:S(2)}) collective-permute-start(f32[2,3,96,128]{3,2,1,0:T(8,128)S(1)} %get-tuple-element.42), channel_id=1, source_target_pairs={{0,8},{1,9},{2,10},{3,11},{4,12},{5,13},{6,14},{7,15},{8,0},{9,1},... | collective-permute-start | bytes 884744 | tf_op jit(solution)/shard_map/ppermute | solution.py:264
  54.1 5.4 %collective-permute-start.1 = (f32[4,3,96,128]{3,2,1,0:T(8,128)S(1)}, f32[4,3,96,128]{3,2,1,0:T(8,128)S(1)}, u32[]{:S(2)}, u32[]{:S(2)}) collective-permute-start(f32[4,3,96,128]{3,2,1,0:T(8,128)S(1)} %get-tuple-element.37), channel_id=1, source_target_pairs={{0,3},{1,0},{2,1},{3,2},{4,7},{5,4},{6,5},{7,6},{8,11},{9,8},{10,9... | collective-permute-start | bytes 1769480 | tf_op jit(solution)/shard_map/ppermute | solution.py:263
  59.5 5.2 %collective-permute-done.7 = f32[2,3,96,128]{3,2,1,0:T(8,128)S(1)} collective-permute-done((f32[2,3,96,128]{3,2,1,0:T(8,128)S(1)}, f32[2,3,96,128]{3,2,1,0:T(8,128)S(1)}, u32[]{:S(2)}, u32[]{:S(2)}) %collective-permute-start.7) | collective-permute-done | bytes 294944 | tf_op jit(solution)/shard_map/ppermute | solution.py:264
  64.7 3.4 %collective-permute-done.5 = f32[2,3,96,128]{3,2,1,0:T(8,128)S(1)} collective-permute-done((f32[2,3,96,128]{3,2,1,0:T(8,128)S(1)}, f32[2,3,96,128]{3,2,1,0:T(8,128)S(1)}, u32[]{:S(2)}, u32[]{:S(2)}) %collective-permute-start.5) | collective-permute-done | bytes 294944 | tf_op jit(solution)/shard_map/ppermute | solution.py:264
  70.3 6.3 %collective-permute-start.8 = (f32[4,3,96,128]{3,2,1,0:T(8,128)}, f32[4,3,96,128]{3,2,1,0:T(8,128)S(1)}, u32[]{:S(2)}, u32[]{:S(2)}) collective-permute-start(f32[4,3,96,128]{3,2,1,0:T(8,128)} %pad_maximum_fusion), channel_id=1, source_target_pairs={{0,2},{1,3},{2,0},{3,1},{4,6},{5,7},{6,4},{7,5},{8,10},{9,11},{10,... | collective-permute-start | bytes 1769480 | tf_op jit(solution)/shard_map/ppermute | solution.py:263
  76.9 3.7 %copy-done.6 = f32[1536,1536]{1,0:T(8,128)S(1)} copy-done((f32[1536,1536]{1,0:T(8,128)S(1)}, f32[1536,1536]{1,0:T(8,128)}, u32[]{:S(2)}) %copy-start.6) | copy-done | bytes 9437208
  80.5 14.2 %shard_map.57 = f32[16,3,96,128]{3,2,1,0:T(8,128)S(1)} custom-call(s32[1]{0:T(128)} %bitcast.block_ref, f32[16,3,96,128]{3,2,1,0:T(8,128)} %all-to-all-done.v_ref, f32[1536,1536]{1,0:T(8,128)S(1)} %copy-done.6, f32[1536,128]{1,0:T(8,128)S(1)} %broadcast_in_dim.2.metric_ref), custom_call_target="tpu_custom_call" | custom-call | flops 5435817984 | bytes 14155776 | tf_op jit(solution)/shard_map/pallas_call | solution.py:170
  94.8 10.5 %collective-permute-done = f32[4,3,96,128]{3,2,1,0:T(8,128)S(1)} collective-permute-done((f32[4,3,96,128]{3,2,1,0:T(8,128)S(1)}, f32[4,3,96,128]{3,2,1,0:T(8,128)S(1)}, u32[]{:S(2)}, u32[]{:S(2)}) %collective-permute-start) | collective-permute-done | bytes 589856 | tf_op jit(solution)/shard_map/ppermute | solution.py:263
  106.1 2.9 %collective-permute-start.4 = (f32[2,3,96,128]{3,2,1,0:T(8,128)}, f32[2,3,96,128]{3,2,1,0:T(8,128)}, u32[]{:S(2)}, u32[]{:S(2)}) collective-permute-start(f32[2,3,96,128]{3,2,1,0:T(8,128)} %get-tuple-element.43), channel_id=1, source_target_pairs={{0,12},{1,13},{2,14},{3,15},{4,0},{5,1},{6,2},{7,3},{8,4},{9,5},{1... | collective-permute-start | bytes 884744 | tf_op jit(solution)/shard_map/ppermute | solution.py:264
  109.1 2.2 %collective-permute-start.3 = (f32[2,3,96,128]{3,2,1,0:T(8,128)}, f32[2,3,96,128]{3,2,1,0:T(8,128)}, u32[]{:S(2)}, u32[]{:S(2)}) collective-permute-start(f32[2,3,96,128]{3,2,1,0:T(8,128)} %get-tuple-element.46), channel_id=1, source_target_pairs={{0,8},{1,9},{2,10},{3,11},{4,12},{5,13},{6,14},{7,15},{8,0},{9,1},... | collective-permute-start | bytes 884744 | tf_op jit(solution)/shard_map/ppermute | solution.py:264
  111.3 3.4 %add.184 = f32[16,3,96,128]{3,2,1,0:T(8,128)} add(f32[16,3,96,128]{3,2,1,0:T(8,128)} %all-to-all-done.1, f32[16,3,96,128]{3,2,1,0:T(8,128)S(1)} %shard_map.57) | non-fusion elementwise | flops 589824 | bytes 7077888 | tf_op jit(solution)/shard_map/add | solution.py:286
  114.7 4.8 %collective-permute-done.8 = f32[4,3,96,128]{3,2,1,0:T(8,128)S(1)} collective-permute-done((f32[4,3,96,128]{3,2,1,0:T(8,128)}, f32[4,3,96,128]{3,2,1,0:T(8,128)S(1)}, u32[]{:S(2)}, u32[]{:S(2)}) %collective-permute-start.8) | collective-permute-done | bytes 589856 | tf_op jit(solution)/shard_map/ppermute | solution.py:263
  121.2 3.4 %collective-permute-done.2 = f32[2,3,96,128]{3,2,1,0:T(8,128)} collective-permute-done((f32[2,3,96,128]{3,2,1,0:T(8,128)}, f32[2,3,96,128]{3,2,1,0:T(8,128)}, u32[]{:S(2)}, u32[]{:S(2)}) %collective-permute-start.2) | collective-permute-done | bytes 294944 | tf_op jit(solution)/shard_map/ppermute | solution.py:264
  124.6 11.6 %all-to-all-start.2 = ((f32[16,3,96,128]{3,2,1,0:T(8,128)}), f32[16,3,96,128]{3,2,1,0:T(8,128)S(1)}, u32[]{:S(2)}, u32[]{:S(2)}) async-start(f32[16,3,96,128]{3,2,1,0:T(8,128)} %add.184), calls=%async_computation.2 | async-start | bytes 4718592 | tf_op jit(solution)/shard_map/all_to_all | solution.py:258
  139.7 5.1 %shard_map.58.w_hbm = f32[3,16,96,128]{3,2,1,0:T(8,128)S(1)} custom-call(s32[16]{0:T(128)S(1)} %stack.101.at_ref, f32[16,3,96,128]{3,2,1,0:T(8,128)S(1)} %constant_dynamic-update-slice_fusion.v_ref, f32[128,128]{1,0:T(8,128)S(1)} %copy-done.5), custom_call_target="tpu_custom_call" | custom-call | flops 452984832 | bytes 4718592 | tf_op jit(solution)/shard_map/pallas_call | solution.py:214
  146.2 49.5 %all-to-all-done.2.a_ref = f32[16,3,96,128]{3,2,1,0:T(8,128)S(1)} async-done(((f32[16,3,96,128]{3,2,1,0:T(8,128)}), f32[16,3,96,128]{3,2,1,0:T(8,128)S(1)}, u32[]{:S(2)}, u32[]{:S(2)}) %all-to-all-start.2) | async-done | bytes 2359328 | tf_op jit(solution)/shard_map/all_to_all | solution.py:258
  197.4 2.7 %shard_map.59 = f32[3,16,96,128]{3,2,1,0:T(8,128)} custom-call(f32[16,3,96,128]{3,2,1,0:T(8,128)S(1)} %all-to-all-done.2.a_ref, f32[3,16,96,128]{3,2,1,0:T(8,128)S(1)} %copy-done.1), custom_call_target="tpu_custom_call" | custom-call | bytes 7077888 | tf_op jit(solution)/shard_map/pallas_call | solution.py:246
  (45 shorter events, 13.0 us)
Async XLA Ops:
  5.3 6.6 %copy-start.2 = (f32[3,8,256,96]{2,3,1,0:T(8,128)S(1)}, f32[3,8,256,96]{2,3,1,0:T(8,128)}, u32[]{:S(2)}) copy-start(f32[3,8,256,96]{2,3,1,0:T(8,128)} %param.5) | copy-start | bytes 7077892
  5.3 6.6 %copy-start.4 = (f32[256,256]{1,0:T(8,128)S(1)}, f32[256,256]{1,0:T(8,128)}, u32[]{:S(2)}) copy-start(f32[256,256]{1,0:T(8,128)} %dx_ref.1) | copy-start | bytes 786436
  5.3 34.9 %all-to-all-start = ((f32[16,3,96,128]{3,2,1,0:T(8,128)}), f32[16,3,96,128]{3,2,1,0:T(8,128)}, u32[]{:S(2)}, u32[]{:S(2)}) async-start(f32[16,3,96,128]{3,2,1,0:T(8,128)} %shard_map.56), calls=%async_computation | async-start | bytes 4718592 | tf_op jit(solution)/shard_map/all_to_all | solution.py:258
  17.1 1.4 copy-start.3
  40.2 71.1 %all-to-all-start.1 = ((f32[16,3,96,128]{3,2,1,0:T(8,128)}), f32[16,3,96,128]{3,2,1,0:T(8,128)}, u32[]{:S(2)}, u32[]{:S(2)}) async-start(f32[16,3,96,128]{3,2,1,0:T(8,128)} %copy-done.3), calls=%async_computation.1 | async-start | bytes 4718592 | tf_op jit(solution)/shard_map/all_to_all | solution.py:258
  49.0 27.6 %copy-start.9 = (f32[1536]{0:T(1024)S(1)}, f32[1536]{0:T(1024)}, u32[]{:S(2)}) copy-start(f32[1536]{0:T(1024)} %param.9) | copy-start | bytes 18436
  49.0 15.7 %collective-permute-start.7 = (f32[2,3,96,128]{3,2,1,0:T(8,128)S(1)}, f32[2,3,96,128]{3,2,1,0:T(8,128)S(1)}, u32[]{:S(2)}, u32[]{:S(2)}) collective-permute-start(f32[2,3,96,128]{3,2,1,0:T(8,128)S(1)} %get-tuple-element.39), channel_id=1, source_target_pairs={{0,12},{1,13},{2,14},{3,15},{4,0},{5,1},{6,2},{7,3},{8,4},{9,5},{1... | collective-permute-start | bytes 884744 | tf_op jit(solution)/shard_map/ppermute | solution.py:264
  51.7 16.3 %collective-permute-start.5 = (f32[2,3,96,128]{3,2,1,0:T(8,128)S(1)}, f32[2,3,96,128]{3,2,1,0:T(8,128)S(1)}, u32[]{:S(2)}, u32[]{:S(2)}) collective-permute-start(f32[2,3,96,128]{3,2,1,0:T(8,128)S(1)} %get-tuple-element.41), channel_id=1, source_target_pairs={{0,4},{1,5},{2,6},{3,7},{4,8},{5,9},{6,10},{7,11},{8,12},{9,13},{1... | collective-permute-start | bytes 884744 | tf_op jit(solution)/shard_map/ppermute | solution.py:264
  51.8 17.0 %collective-permute-start.6 = (f32[2,3,96,128]{3,2,1,0:T(8,128)S(1)}, f32[2,3,96,128]{3,2,1,0:T(8,128)S(1)}, u32[]{:S(2)}, u32[]{:S(2)}) collective-permute-start(f32[2,3,96,128]{3,2,1,0:T(8,128)S(1)} %get-tuple-element.42), channel_id=1, source_target_pairs={{0,8},{1,9},{2,10},{3,11},{4,12},{5,13},{6,14},{7,15},{8,0},{9,1},... | collective-permute-start | bytes 884744 | tf_op jit(solution)/shard_map/ppermute | solution.py:264
  54.1 40.7 %collective-permute-start.1 = (f32[4,3,96,128]{3,2,1,0:T(8,128)S(1)}, f32[4,3,96,128]{3,2,1,0:T(8,128)S(1)}, u32[]{:S(2)}, u32[]{:S(2)}) collective-permute-start(f32[4,3,96,128]{3,2,1,0:T(8,128)S(1)} %get-tuple-element.37), channel_id=1, source_target_pairs={{0,3},{1,0},{2,1},{3,2},{4,7},{5,4},{6,5},{7,6},{8,11},{9,8},{10,9... | collective-permute-start | bytes 1769480 | tf_op jit(solution)/shard_map/ppermute | solution.py:263
  59.5 45.8 %collective-permute-start = (f32[4,3,96,128]{3,2,1,0:T(8,128)S(1)}, f32[4,3,96,128]{3,2,1,0:T(8,128)S(1)}, u32[]{:S(2)}, u32[]{:S(2)}) collective-permute-start(f32[4,3,96,128]{3,2,1,0:T(8,128)S(1)} %get-tuple-element.38), channel_id=1, source_target_pairs={{0,1},{1,2},{2,3},{3,0},{4,5},{5,6},{6,7},{7,4},{8,9},{9,10},{10,1... | collective-permute-start | bytes 1769480 | tf_op jit(solution)/shard_map/ppermute | solution.py:263
  70.3 49.2 %collective-permute-start.8 = (f32[4,3,96,128]{3,2,1,0:T(8,128)}, f32[4,3,96,128]{3,2,1,0:T(8,128)S(1)}, u32[]{:S(2)}, u32[]{:S(2)}) collective-permute-start(f32[4,3,96,128]{3,2,1,0:T(8,128)} %pad_maximum_fusion), channel_id=1, source_target_pairs={{0,2},{1,3},{2,0},{3,1},{4,6},{5,7},{6,4},{7,5},{8,10},{9,11},{10,... | collective-permute-start | bytes 1769480 | tf_op jit(solution)/shard_map/ppermute | solution.py:263
  76.8 3.7 %copy-start.6 = (f32[1536,1536]{1,0:T(8,128)S(1)}, f32[1536,1536]{1,0:T(8,128)}, u32[]{:S(2)}) copy-start(f32[1536,1536]{1,0:T(8,128)} %dy_ref.1) | copy-start | bytes 28311556
  106.1 15.1 %collective-permute-start.4 = (f32[2,3,96,128]{3,2,1,0:T(8,128)}, f32[2,3,96,128]{3,2,1,0:T(8,128)}, u32[]{:S(2)}, u32[]{:S(2)}) collective-permute-start(f32[2,3,96,128]{3,2,1,0:T(8,128)} %get-tuple-element.43), channel_id=1, source_target_pairs={{0,12},{1,13},{2,14},{3,15},{4,0},{5,1},{6,2},{7,3},{8,4},{9,5},{1... | collective-permute-start | bytes 884744 | tf_op jit(solution)/shard_map/ppermute | solution.py:264
  109.0 15.6 %collective-permute-start.2 = (f32[2,3,96,128]{3,2,1,0:T(8,128)}, f32[2,3,96,128]{3,2,1,0:T(8,128)}, u32[]{:S(2)}, u32[]{:S(2)}) collective-permute-start(f32[2,3,96,128]{3,2,1,0:T(8,128)} %get-tuple-element.45), channel_id=1, source_target_pairs={{0,4},{1,5},{2,6},{3,7},{4,8},{5,9},{6,10},{7,11},{8,12},{9,13},{1... | collective-permute-start | bytes 884744 | tf_op jit(solution)/shard_map/ppermute | solution.py:264
  109.1 15.6 %collective-permute-start.3 = (f32[2,3,96,128]{3,2,1,0:T(8,128)}, f32[2,3,96,128]{3,2,1,0:T(8,128)}, u32[]{:S(2)}, u32[]{:S(2)}) collective-permute-start(f32[2,3,96,128]{3,2,1,0:T(8,128)} %get-tuple-element.46), channel_id=1, source_target_pairs={{0,8},{1,9},{2,10},{3,11},{4,12},{5,13},{6,14},{7,15},{8,0},{9,1},... | collective-permute-start | bytes 884744 | tf_op jit(solution)/shard_map/ppermute | solution.py:264
  124.6 71.1 %all-to-all-start.2 = ((f32[16,3,96,128]{3,2,1,0:T(8,128)}), f32[16,3,96,128]{3,2,1,0:T(8,128)S(1)}, u32[]{:S(2)}, u32[]{:S(2)}) async-start(f32[16,3,96,128]{3,2,1,0:T(8,128)} %add.184), calls=%async_computation.2 | async-start | bytes 4718592 | tf_op jit(solution)/shard_map/all_to_all | solution.py:258
  136.4 3.1 %copy-start.7 = (f32[3,96,128]{2,1,0:T(8,128)S(1)}, f32[3,96,128]{2,1,0:T(8,128)}, u32[]{:S(2)}) copy-start(f32[3,96,128]{2,1,0:T(8,128)} %get-tuple-element.31) | copy-start | bytes 442372
  136.5 3.1 %copy-start.8 = (f32[3,96,128]{2,1,0:T(8,128)S(1)}, f32[3,96,128]{2,1,0:T(8,128)}, u32[]{:S(2)}) copy-start(f32[3,96,128]{2,1,0:T(8,128)} %get-tuple-element.32) | copy-start | bytes 442372
  136.5 3.2 %copy-start.5 = (f32[128,128]{1,0:T(8,128)S(1)}, f32[128,128]{1,0:T(8,128)}, u32[]{:S(2)}) copy-start(f32[128,128]{1,0:T(8,128)} %dz_ref.1) | copy-start | bytes 196612
  144.8 1.4 copy-start
  195.7 1.7 copy-start.1

commit v4 on v3

--- a/solution.py
+++ b/solution.py
@@ -28,17 +28,6 @@
     return lax.broadcasted_iota(jnp.int32, (8, LN), 1)
 
 
-def swap_bits(arrs, dist, shift, lane):
-    low = (lane & shift) == 0
-    out = list(arrs)
-    for i in range(len(arrs)):
-        if i & dist == 0:
-            a, b = arrs[i], arrs[i | dist]
-            out[i] = jnp.where(low, a, pltpu.roll(b, shift, 1))
-            out[i | dist] = jnp.where(low, pltpu.roll(a, LN - shift, 1), b)
-    return out
-
-
 def zx_to_xz(lane, block):
     lane = (lane - 8 * block) & (LN - 1)
     return ((lane & 7) << 4) | (lane & 8) | (lane >> 4)
@@ -67,11 +56,19 @@
     return dot(a[0], b[0]) + (dot(a[0], b[1]) + dot(a[1], b[0]))
 
 
+def turn(arrs, width, lane):
+    n = len(arrs)
+    step = 1
+    while step < n:
+        high = (lane & width * step) != 0
+        arrs = [jnp.where(high, arrs[(i + step) % n], arrs[i]) for i in range(n)]
+        step *= 2
+    return [pltpu.roll(arrs[-g % n], LN - width * g, 1) if g else arrs[0] for g in range(n)]
+
+
 def x_to_blocks(load, lane, half):
     arrs = [load(z, half) for z in range(ZB)]
-    for k in (2, 1, 0):
-        arrs = swap_bits(arrs, 1 << k, 16 << k, lane)
-    return arrs
+    return turn([pltpu.roll(a, 16 * z, 1) if z else a for z, a in enumerate(arrs)], 16, lane)
 
 
 def pack_kernel(v_hbm, out_hbm, v_ref, out_ref, sems):
@@ -186,10 +183,7 @@
 
 
 def z_to_lanes(arrs, lane):
-    for k in range(4):
-        high = (lane & 8 << k) != 0
-        arrs = [jnp.where(high, arrs[(i + (1 << k)) % NB], arrs[i]) for i in range(NB)]
-    turned = [pltpu.roll(arrs[-g % NB], (LN - 8 * g) % LN, 1) if g else arrs[0] for g in range(NB)]
+    turned = turn(arrs, 8, lane)
     return [turned[(x & 7) * 2 + (x >> 3)] for x in range(NB)]
 
 

time: 201 us -> 200 us (level)
  no operation moved by 1% of the time
where the time goes in v4:
time: 200 us; the launch traced here: 199 us
  waiting for transfers between devices  101 us (50%)
  starting transfers between devices  47 us (24%)
  Pallas kernels  30.7 us (15%)
  local copies, waits for them, and re-layouts  14.8 us (7%)
  other arithmetic  5.33 us (3%)
    all_to_all x3, waiting for transfers between devices, exchange(): return lax.all_to_all(a, axis, split_axis=0, concat_axis=0, tiled=True)  72 us
    all_to_all x3, starting transfers between devices, exchange(): return lax.all_to_all(a, axis, split_axis=0, concat_axis=0, tiled=True)  25.2 us
    ppermute x3, waiting for transfers between devices, col_exchange(): lax.ppermute(x, 'col', [(i * 4 + j, i * 4 + (j + s) % 4) for i in range(4...  15.3 us
    pallas_call x1, Pallas kernels, y_term(): call(y_kernel, 6 * NY * NY * NC * LN, 2 * SIZE + NY * NY * 4, grid=(NB //...  14.2 us
    ppermute x6, waiting for transfers between devices, col_exchange(): lax.ppermute(x, 'col', [(i * 4 + j, (i + s) % 4 * 4 + j) for i in range(4...  13.7 us
    ppermute x3, starting transfers between devices, col_exchange(): lax.ppermute(x, 'col', [(i * 4 + j, i * 4 + (j + s) % 4) for i in range(4...  11.7 us
    unnamed x28, local copies, waits for them, and re-layouts  11.3 us
    ppermute x6, starting transfers between devices, col_exchange(): lax.ppermute(x, 'col', [(i * 4 + j, (i + s) % 4 * 4 + j) for i in range(4...  10.2 us
  transfers between devices with their start and end apart: 12, of which 8 were waited for; matrix products, arithmetic and copies ran while one was open for 6% of the time, Pallas kernels for 12%

profile of v4, /device:TPU:4, one launch (start us, length us, event | category | flops | bytes accessed | tf_op | source)
XLA Modules:
  0.0 199.2 jit_solution(9011908600454541724)
XLA Ops:
  0.0 4.4 %shard_map.56 = f32[16,3,96,128]{3,2,1,0:T(8,128)} custom-call(f32[3,8,96,256]{3,2,1,0:T(8,128)} %bitcast.58), custom_call_target="tpu_custom_call" | custom-call | bytes 4718592 | tf_op jit(solution)/shard_map/pallas_call | solution.py:96
  4.4 6.6 %all-to-all-start = ((f32[16,3,96,128]{3,2,1,0:T(8,128)}), f32[16,3,96,128]{3,2,1,0:T(8,128)}, u32[]{:S(2)}, u32[]{:S(2)}) async-start(f32[16,3,96,128]{3,2,1,0:T(8,128)} %shard_map.56), calls=%async_computation | async-start | bytes 4718592 | tf_op jit(solution)/shard_map/all_to_all | solution.py:252
  11.0 4.3 %shard_map.55 = f32[16,3,96,128]{3,2,1,0:T(8,128)S(1)} custom-call(s32[1]{0:T(128)} %bitcast.block_ref, f32[3,8,96,256]{3,2,1,0:T(8,128)S(1)} %bitcast.59, f32[256,256]{1,0:T(8,128)S(1)} %copy-done.4), custom_call_target="tpu_custom_call" | custom-call | flops 905969664 | bytes 4718592 | tf_op jit(solution)/shard_map/pallas_call | solution.py:130
  16.7 22.5 %all-to-all-done.v_ref = f32[16,3,96,128]{3,2,1,0:T(8,128)} async-done(((f32[16,3,96,128]{3,2,1,0:T(8,128)}), f32[16,3,96,128]{3,2,1,0:T(8,128)}, u32[]{:S(2)}, u32[]{:S(2)}) %all-to-all-start) | async-done | bytes 2359328 | tf_op jit(solution)/shard_map/all_to_all | solution.py:252
  39.3 6.9 %all-to-all-start.1 = ((f32[16,3,96,128]{3,2,1,0:T(8,128)}), f32[16,3,96,128]{3,2,1,0:T(8,128)}, u32[]{:S(2)}, u32[]{:S(2)}) async-start(f32[16,3,96,128]{3,2,1,0:T(8,128)} %copy-done.3), calls=%async_computation.1 | async-start | bytes 4718592 | tf_op jit(solution)/shard_map/all_to_all | solution.py:252
  46.2 1.8 constant_dynamic-slice_fusion
  48.1 2.7 %collective-permute-start.7 = (f32[2,3,96,128]{3,2,1,0:T(8,128)S(1)}, f32[2,3,96,128]{3,2,1,0:T(8,128)S(1)}, u32[]{:S(2)}, u32[]{:S(2)}) collective-permute-start(f32[2,3,96,128]{3,2,1,0:T(8,128)S(1)} %get-tuple-element.39), channel_id=1, source_target_pairs={{0,12},{1,13},{2,14},{3,15},{4,0},{5,1},{6,2},{7,3},{8,4},{9,5},{1... | collective-permute-start | bytes 884744 | tf_op jit(solution)/shard_map/ppermute | solution.py:258
  50.9 2.3 %collective-permute-start.6 = (f32[2,3,96,128]{3,2,1,0:T(8,128)S(1)}, f32[2,3,96,128]{3,2,1,0:T(8,128)S(1)}, u32[]{:S(2)}, u32[]{:S(2)}) collective-permute-start(f32[2,3,96,128]{3,2,1,0:T(8,128)S(1)} %get-tuple-element.42), channel_id=1, source_target_pairs={{0,8},{1,9},{2,10},{3,11},{4,12},{5,13},{6,14},{7,15},{8,0},{9,1},... | collective-permute-start | bytes 884744 | tf_op jit(solution)/shard_map/ppermute | solution.py:258
  53.1 5.4 %collective-permute-start.1 = (f32[4,3,96,128]{3,2,1,0:T(8,128)S(1)}, f32[4,3,96,128]{3,2,1,0:T(8,128)S(1)}, u32[]{:S(2)}, u32[]{:S(2)}) collective-permute-start(f32[4,3,96,128]{3,2,1,0:T(8,128)S(1)} %get-tuple-element.37), channel_id=1, source_target_pairs={{0,3},{1,0},{2,1},{3,2},{4,7},{5,4},{6,5},{7,6},{8,11},{9,8},{10,9... | collective-permute-start | bytes 1769480 | tf_op jit(solution)/shard_map/ppermute | solution.py:257
  58.6 5.2 %collective-permute-done.7 = f32[2,3,96,128]{3,2,1,0:T(8,128)S(1)} collective-permute-done((f32[2,3,96,128]{3,2,1,0:T(8,128)S(1)}, f32[2,3,96,128]{3,2,1,0:T(8,128)S(1)}, u32[]{:S(2)}, u32[]{:S(2)}) %collective-permute-start.7) | collective-permute-done | bytes 294944 | tf_op jit(solution)/shard_map/ppermute | solution.py:258
  63.8 3.4 %collective-permute-done.5 = f32[2,3,96,128]{3,2,1,0:T(8,128)S(1)} collective-permute-done((f32[2,3,96,128]{3,2,1,0:T(8,128)S(1)}, f32[2,3,96,128]{3,2,1,0:T(8,128)S(1)}, u32[]{:S(2)}, u32[]{:S(2)}) %collective-permute-start.5) | collective-permute-done | bytes 294944 | tf_op jit(solution)/shard_map/ppermute | solution.py:258
  69.4 6.3 %collective-permute-start.8 = (f32[4,3,96,128]{3,2,1,0:T(8,128)}, f32[4,3,96,128]{3,2,1,0:T(8,128)S(1)}, u32[]{:S(2)}, u32[]{:S(2)}) collective-permute-start(f32[4,3,96,128]{3,2,1,0:T(8,128)} %pad_maximum_fusion), channel_id=1, source_target_pairs={{0,2},{1,3},{2,0},{3,1},{4,6},{5,7},{6,4},{7,5},{8,10},{9,11},{10,... | collective-permute-start | bytes 1769480 | tf_op jit(solution)/shard_map/ppermute | solution.py:257
  76.0 3.7 %copy-done.6 = f32[1536,1536]{1,0:T(8,128)S(1)} copy-done((f32[1536,1536]{1,0:T(8,128)S(1)}, f32[1536,1536]{1,0:T(8,128)}, u32[]{:S(2)}) %copy-start.6) | copy-done | bytes 9437208
  79.6 14.2 %shard_map.57 = f32[16,3,96,128]{3,2,1,0:T(8,128)S(1)} custom-call(s32[1]{0:T(128)} %bitcast.block_ref, f32[16,3,96,128]{3,2,1,0:T(8,128)} %all-to-all-done.v_ref, f32[1536,1536]{1,0:T(8,128)S(1)} %copy-done.6, f32[1536,128]{1,0:T(8,128)S(1)} %broadcast_in_dim.2.metric_ref), custom_call_target="tpu_custom_call" | custom-call | flops 5435817984 | bytes 14155776 | tf_op jit(solution)/shard_map/pallas_call | solution.py:167
  93.9 10.5 %collective-permute-done = f32[4,3,96,128]{3,2,1,0:T(8,128)S(1)} collective-permute-done((f32[4,3,96,128]{3,2,1,0:T(8,128)S(1)}, f32[4,3,96,128]{3,2,1,0:T(8,128)S(1)}, u32[]{:S(2)}, u32[]{:S(2)}) %collective-permute-start) | collective-permute-done | bytes 589856 | tf_op jit(solution)/shard_map/ppermute | solution.py:257
  105.2 2.9 %collective-permute-start.4 = (f32[2,3,96,128]{3,2,1,0:T(8,128)}, f32[2,3,96,128]{3,2,1,0:T(8,128)}, u32[]{:S(2)}, u32[]{:S(2)}) collective-permute-start(f32[2,3,96,128]{3,2,1,0:T(8,128)} %get-tuple-element.43), channel_id=1, source_target_pairs={{0,12},{1,13},{2,14},{3,15},{4,0},{5,1},{6,2},{7,3},{8,4},{9,5},{1... | collective-permute-start | bytes 884744 | tf_op jit(solution)/shard_map/ppermute | solution.py:258
  108.1 2.2 %collective-permute-start.3 = (f32[2,3,96,128]{3,2,1,0:T(8,128)}, f32[2,3,96,128]{3,2,1,0:T(8,128)}, u32[]{:S(2)}, u32[]{:S(2)}) collective-permute-start(f32[2,3,96,128]{3,2,1,0:T(8,128)} %get-tuple-element.46), channel_id=1, source_target_pairs={{0,8},{1,9},{2,10},{3,11},{4,12},{5,13},{6,14},{7,15},{8,0},{9,1},... | collective-permute-start | bytes 884744 | tf_op jit(solution)/shard_map/ppermute | solution.py:258
  110.4 3.4 %add.184 = f32[16,3,96,128]{3,2,1,0:T(8,128)} add(f32[16,3,96,128]{3,2,1,0:T(8,128)} %all-to-all-done.1, f32[16,3,96,128]{3,2,1,0:T(8,128)S(1)} %shard_map.57) | non-fusion elementwise | flops 589824 | bytes 7077888 | tf_op jit(solution)/shard_map/add | solution.py:280
  113.8 4.8 %collective-permute-done.8 = f32[4,3,96,128]{3,2,1,0:T(8,128)S(1)} collective-permute-done((f32[4,3,96,128]{3,2,1,0:T(8,128)}, f32[4,3,96,128]{3,2,1,0:T(8,128)S(1)}, u32[]{:S(2)}, u32[]{:S(2)}) %collective-permute-start.8) | collective-permute-done | bytes 589856 | tf_op jit(solution)/shard_map/ppermute | solution.py:257
  120.3 3.4 %collective-permute-done.2 = f32[2,3,96,128]{3,2,1,0:T(8,128)} collective-permute-done((f32[2,3,96,128]{3,2,1,0:T(8,128)}, f32[2,3,96,128]{3,2,1,0:T(8,128)}, u32[]{:S(2)}, u32[]{:S(2)}) %collective-permute-start.2) | collective-permute-done | bytes 294944 | tf_op jit(solution)/shard_map/ppermute | solution.py:258
  123.7 11.6 %all-to-all-start.2 = ((f32[16,3,96,128]{3,2,1,0:T(8,128)}), f32[16,3,96,128]{3,2,1,0:T(8,128)S(1)}, u32[]{:S(2)}, u32[]{:S(2)}) async-start(f32[16,3,96,128]{3,2,1,0:T(8,128)} %add.184), calls=%async_computation.2 | async-start | bytes 4718592 | tf_op jit(solution)/shard_map/all_to_all | solution.py:252
  138.8 5.1 %shard_map.58.w_hbm = f32[3,16,96,128]{3,2,1,0:T(8,128)S(1)} custom-call(s32[16]{0:T(128)S(1)} %stack.101.at_ref, f32[16,3,96,128]{3,2,1,0:T(8,128)S(1)} %constant_dynamic-update-slice_fusion.v_ref, f32[128,128]{1,0:T(8,128)S(1)} %copy-done.5), custom_call_target="tpu_custom_call" | custom-call | flops 452984832 | bytes 4718592 | tf_op jit(solution)/shard_map/pallas_call | solution.py:208
  145.3 49.5 %all-to-all-done.2.a_ref = f32[16,3,96,128]{3,2,1,0:T(8,128)S(1)} async-done(((f32[16,3,96,128]{3,2,1,0:T(8,128)}), f32[16,3,96,128]{3,2,1,0:T(8,128)S(1)}, u32[]{:S(2)}, u32[]{:S(2)}) %all-to-all-start.2) | async-done | bytes 2359328 | tf_op jit(solution)/shard_map/all_to_all | solution.py:252
  196.5 2.7 %shard_map.59 = f32[3,16,96,128]{3,2,1,0:T(8,128)} custom-call(f32[16,3,96,128]{3,2,1,0:T(8,128)S(1)} %all-to-all-done.2.a_ref, f32[3,16,96,128]{3,2,1,0:T(8,128)S(1)} %copy-done.1), custom_call_target="tpu_custom_call" | custom-call | bytes 7077888 | tf_op jit(solution)/shard_map/pallas_call | solution.py:240
  (45 shorter events, 13.0 us)
Async XLA Ops:
  4.4 6.6 %copy-start.2 = (f32[3,8,256,96]{2,3,1,0:T(8,128)S(1)}, f32[3,8,256,96]{2,3,1,0:T(8,128)}, u32[]{:S(2)}) copy-start(f32[3,8,256,96]{2,3,1,0:T(8,128)} %param.5) | copy-start | bytes 7077892
  4.4 6.6 %copy-start.4 = (f32[256,256]{1,0:T(8,128)S(1)}, f32[256,256]{1,0:T(8,128)}, u32[]{:S(2)}) copy-start(f32[256,256]{1,0:T(8,128)} %dx_ref.1) | copy-start | bytes 786436
  4.4 34.9 %all-to-all-start = ((f32[16,3,96,128]{3,2,1,0:T(8,128)}), f32[16,3,96,128]{3,2,1,0:T(8,128)}, u32[]{:S(2)}, u32[]{:S(2)}) async-start(f32[16,3,96,128]{3,2,1,0:T(8,128)} %shard_map.56), calls=%async_computation | async-start | bytes 4718592 | tf_op jit(solution)/shard_map/all_to_all | solution.py:252
  15.3 1.4 copy-start.3
  39.3 71.1 %all-to-all-start.1 = ((f32[16,3,96,128]{3,2,1,0:T(8,128)}), f32[16,3,96,128]{3,2,1,0:T(8,128)}, u32[]{:S(2)}, u32[]{:S(2)}) async-start(f32[16,3,96,128]{3,2,1,0:T(8,128)} %copy-done.3), calls=%async_computation.1 | async-start | bytes 4718592 | tf_op jit(solution)/shard_map/all_to_all | solution.py:252
  48.1 27.6 %copy-start.9 = (f32[1536]{0:T(1024)S(1)}, f32[1536]{0:T(1024)}, u32[]{:S(2)}) copy-start(f32[1536]{0:T(1024)} %param.9) | copy-start | bytes 18436
  48.1 15.7 %collective-permute-start.7 = (f32[2,3,96,128]{3,2,1,0:T(8,128)S(1)}, f32[2,3,96,128]{3,2,1,0:T(8,128)S(1)}, u32[]{:S(2)}, u32[]{:S(2)}) collective-permute-start(f32[2,3,96,128]{3,2,1,0:T(8,128)S(1)} %get-tuple-element.39), channel_id=1, source_target_pairs={{0,12},{1,13},{2,14},{3,15},{4,0},{5,1},{6,2},{7,3},{8,4},{9,5},{1... | collective-permute-start | bytes 884744 | tf_op jit(solution)/shard_map/ppermute | solution.py:258
  50.8 16.3 %collective-permute-start.5 = (f32[2,3,96,128]{3,2,1,0:T(8,128)S(1)}, f32[2,3,96,128]{3,2,1,0:T(8,128)S(1)}, u32[]{:S(2)}, u32[]{:S(2)}) collective-permute-start(f32[2,3,96,128]{3,2,1,0:T(8,128)S(1)} %get-tuple-element.41), channel_id=1, source_target_pairs={{0,4},{1,5},{2,6},{3,7},{4,8},{5,9},{6,10},{7,11},{8,12},{9,13},{1... | collective-permute-start | bytes 884744 | tf_op jit(solution)/shard_map/ppermute | solution.py:258
  50.9 17.0 %collective-permute-start.6 = (f32[2,3,96,128]{3,2,1,0:T(8,128)S(1)}, f32[2,3,96,128]{3,2,1,0:T(8,128)S(1)}, u32[]{:S(2)}, u32[]{:S(2)}) collective-permute-start(f32[2,3,96,128]{3,2,1,0:T(8,128)S(1)} %get-tuple-element.42), channel_id=1, source_target_pairs={{0,8},{1,9},{2,10},{3,11},{4,12},{5,13},{6,14},{7,15},{8,0},{9,1},... | collective-permute-start | bytes 884744 | tf_op jit(solution)/shard_map/ppermute | solution.py:258
  53.1 40.7 %collective-permute-start.1 = (f32[4,3,96,128]{3,2,1,0:T(8,128)S(1)}, f32[4,3,96,128]{3,2,1,0:T(8,128)S(1)}, u32[]{:S(2)}, u32[]{:S(2)}) collective-permute-start(f32[4,3,96,128]{3,2,1,0:T(8,128)S(1)} %get-tuple-element.37), channel_id=1, source_target_pairs={{0,3},{1,0},{2,1},{3,2},{4,7},{5,4},{6,5},{7,6},{8,11},{9,8},{10,9... | collective-permute-start | bytes 1769480 | tf_op jit(solution)/shard_map/ppermute | solution.py:257
  58.5 45.8 %collective-permute-start = (f32[4,3,96,128]{3,2,1,0:T(8,128)S(1)}, f32[4,3,96,128]{3,2,1,0:T(8,128)S(1)}, u32[]{:S(2)}, u32[]{:S(2)}) collective-permute-start(f32[4,3,96,128]{3,2,1,0:T(8,128)S(1)} %get-tuple-element.38), channel_id=1, source_target_pairs={{0,1},{1,2},{2,3},{3,0},{4,5},{5,6},{6,7},{7,4},{8,9},{9,10},{10,1... | collective-permute-start | bytes 1769480 | tf_op jit(solution)/shard_map/ppermute | solution.py:257
  69.4 49.2 %collective-permute-start.8 = (f32[4,3,96,128]{3,2,1,0:T(8,128)}, f32[4,3,96,128]{3,2,1,0:T(8,128)S(1)}, u32[]{:S(2)}, u32[]{:S(2)}) collective-permute-start(f32[4,3,96,128]{3,2,1,0:T(8,128)} %pad_maximum_fusion), channel_id=1, source_target_pairs={{0,2},{1,3},{2,0},{3,1},{4,6},{5,7},{6,4},{7,5},{8,10},{9,11},{10,... | collective-permute-start | bytes 1769480 | tf_op jit(solution)/shard_map/ppermute | solution.py:257
  75.9 3.7 %copy-start.6 = (f32[1536,1536]{1,0:T(8,128)S(1)}, f32[1536,1536]{1,0:T(8,128)}, u32[]{:S(2)}) copy-start(f32[1536,1536]{1,0:T(8,128)} %dy_ref.1) | copy-start | bytes 28311556
  105.2 15.1 %collective-permute-start.4 = (f32[2,3,96,128]{3,2,1,0:T(8,128)}, f32[2,3,96,128]{3,2,1,0:T(8,128)}, u32[]{:S(2)}, u32[]{:S(2)}) collective-permute-start(f32[2,3,96,128]{3,2,1,0:T(8,128)} %get-tuple-element.43), channel_id=1, source_target_pairs={{0,12},{1,13},{2,14},{3,15},{4,0},{5,1},{6,2},{7,3},{8,4},{9,5},{1... | collective-permute-start | bytes 884744 | tf_op jit(solution)/shard_map/ppermute | solution.py:258
  108.1 15.6 %collective-permute-start.2 = (f32[2,3,96,128]{3,2,1,0:T(8,128)}, f32[2,3,96,128]{3,2,1,0:T(8,128)}, u32[]{:S(2)}, u32[]{:S(2)}) collective-permute-start(f32[2,3,96,128]{3,2,1,0:T(8,128)} %get-tuple-element.45), channel_id=1, source_target_pairs={{0,4},{1,5},{2,6},{3,7},{4,8},{5,9},{6,10},{7,11},{8,12},{9,13},{1... | collective-permute-start | bytes 884744 | tf_op jit(solution)/shard_map/ppermute | solution.py:258
  108.1 15.6 %collective-permute-start.3 = (f32[2,3,96,128]{3,2,1,0:T(8,128)}, f32[2,3,96,128]{3,2,1,0:T(8,128)}, u32[]{:S(2)}, u32[]{:S(2)}) collective-permute-start(f32[2,3,96,128]{3,2,1,0:T(8,128)} %get-tuple-element.46), channel_id=1, source_target_pairs={{0,8},{1,9},{2,10},{3,11},{4,12},{5,13},{6,14},{7,15},{8,0},{9,1},... | collective-permute-start | bytes 884744 | tf_op jit(solution)/shard_map/ppermute | solution.py:258
  123.7 71.1 %all-to-all-start.2 = ((f32[16,3,96,128]{3,2,1,0:T(8,128)}), f32[16,3,96,128]{3,2,1,0:T(8,128)S(1)}, u32[]{:S(2)}, u32[]{:S(2)}) async-start(f32[16,3,96,128]{3,2,1,0:T(8,128)} %add.184), calls=%async_computation.2 | async-start | bytes 4718592 | tf_op jit(solution)/shard_map/all_to_all | solution.py:252
  135.5 3.1 %copy-start.7 = (f32[3,96,128]{2,1,0:T(8,128)S(1)}, f32[3,96,128]{2,1,0:T(8,128)}, u32[]{:S(2)}) copy-start(f32[3,96,128]{2,1,0:T(8,128)} %get-tuple-element.31) | copy-start | bytes 442372
  135.5 3.1 %copy-start.8 = (f32[3,96,128]{2,1,0:T(8,128)S(1)}, f32[3,96,128]{2,1,0:T(8,128)}, u32[]{:S(2)}) copy-start(f32[3,96,128]{2,1,0:T(8,128)} %get-tuple-element.32) | copy-start | bytes 442372
  135.6 3.2 %copy-start.5 = (f32[128,128]{1,0:T(8,128)S(1)}, f32[128,128]{1,0:T(8,128)}, u32[]{:S(2)}) copy-start(f32[128,128]{1,0:T(8,128)} %dz_ref.1) | copy-start | bytes 196612
  143.9 1.4 copy-start
  194.8 1.7 copy-start.1

commit v5 on v4

--- a/solution.py
+++ b/solution.py
@@ -9,6 +9,7 @@
 ZB, NX, NY = 8, 256, 1536
 SIZE = NB * NC * YB * LN * 4
 BLOCKS = jax.ShapeDtypeStruct((NB, NC, YB, LN), jnp.float32)
+TERMS = jax.ShapeDtypeStruct((28 * NC, NB, YB, LN), jnp.float32)
 PENCILS = jax.ShapeDtypeStruct((NC, NB, YB, LN), jnp.float32)
 VMEM = pl.BlockSpec(memory_space=pltpu.VMEM)
 SMEM = pl.BlockSpec(memory_space=pltpu.SMEM)
@@ -187,7 +188,7 @@
     return [turned[(x & 7) * 2 + (x >> 3)] for x in range(NB)]
 
 
-def z_kernel(at_ref, v_ref, dz_ref, out_ref, t_ref):
+def z_kernel(at_ref, v_ref, dz_ref, out_hbm, t_ref, out_ref, sems):
     d = split(dz_ref[...])
     lane = lanes8()
     at = [at_ref[s] for s in range(NB)]
@@ -199,9 +200,14 @@
             t_ref[c, x, rows, :] = arrs[x]
 
     over_rows(ALL, body)
-    for c in range(NC):
+    stores = []
+    for c in ALL:
         deriv = dot3(split(t_ref[c].reshape(NB * YB, LN)), d, ((1,), (1,)))
         out_ref[c] = t_ref[2] * deriv.reshape(NB, YB, LN)
+        stores.append(pltpu.make_async_copy(out_ref.at[c], out_hbm.at[c], sems.at[c]))
+        stores[c].start()
+    for store in stores:
+        store.wait()
 
 
 def z_term(at, v_z, dz_matrix):
@@ -210,9 +216,9 @@
         6 * NC * NB * YB * LN * LN,
         2 * SIZE,
         in_specs=[SMEM, VMEM, VMEM],
-        out_specs=VMEM,
-        out_shape=PENCILS,
-        scratch_shapes=[pltpu.VMEM((NC, NB, YB, LN), jnp.float32)],
+        out_specs=HBM,
+        out_shape=TERMS,
+        scratch_shapes=[pltpu.VMEM(PENCILS.shape, jnp.float32)] * 2 + [pltpu.SemaphoreType.DMA((NC,))],
     )(at, v_z, dz_matrix)
 
 

time: 200 us -> 199 us (level)
  local copies, waits for them, and re-layouts: 14.8 us -> 11.8 us
  Pallas kernels: 30.7 us -> 32.9 us
    unnamed x28 -> x24, local copies, waits for them, and re-layouts: 11.3 us -> 8.21 us
  transfers between devices with their start and end apart: 12 -> 12, of which waited for: 8 -> 8; matrix products, arithmetic and copies ran while one was open for 6% -> 6% of each run, Pallas kernels for 12% -> 13%
where the time goes in v5:
time: 199 us; the launch traced here: 198 us
  waiting for transfers between devices  101 us (51%)
  starting transfers between devices  47 us (24%)
  Pallas kernels  32.9 us (17%)
  local copies, waits for them, and re-layouts  11.8 us (6%)
  other arithmetic  5.33 us (3%)
    all_to_all x3, waiting for transfers between devices, exchange(): return lax.all_to_all(a, axis, split_axis=0, concat_axis=0, tiled=True)  72.2 us
    all_to_all x3, starting transfers between devices, exchange(): return lax.all_to_all(a, axis, split_axis=0, concat_axis=0, tiled=True)  25.2 us
    ppermute x3, waiting for transfers between devices, col_exchange(): lax.ppermute(x, 'col', [(i * 4 + j, i * 4 + (j + s) % 4) for i in range(4...  15.3 us
    pallas_call x1, Pallas kernels, y_term(): call(y_kernel, 6 * NY * NY * NC * LN, 2 * SIZE + NY * NY * 4, grid=(NB //...  14.2 us
    ppermute x6, waiting for transfers between devices, col_exchange(): lax.ppermute(x, 'col', [(i * 4 + j, (i + s) % 4 * 4 + j) for i in range(4...  13.7 us
    ppermute x3, starting transfers between devices, col_exchange(): lax.ppermute(x, 'col', [(i * 4 + j, i * 4 + (j + s) % 4) for i in range(4...  11.7 us
    ppermute x6, starting transfers between devices, col_exchange(): lax.ppermute(x, 'col', [(i * 4 + j, (i + s) % 4 * 4 + j) for i in range(4...  10.2 us
    unnamed x24, local copies, waits for them, and re-layouts  8.21 us
  transfers between devices with their start and end apart: 12, of which 8 were waited for; matrix products, arithmetic and copies ran while one was open for 6% of the time, Pallas kernels for 13%

profile of v5, /device:TPU:4, one launch (start us, length us, event | category | flops | bytes accessed | tf_op | source)
XLA Modules:
  0.0 198.5 jit_solution(14845384026410097795)
XLA Ops:
  0.0 4.4 %shard_map.56 = f32[16,3,96,128]{3,2,1,0:T(8,128)} custom-call(f32[3,8,96,256]{3,2,1,0:T(8,128)} %bitcast.58), custom_call_target="tpu_custom_call" | custom-call | bytes 4718592 | tf_op jit(solution)/shard_map/pallas_call | solution.py:97
  4.4 6.6 %all-to-all-start = ((f32[16,3,96,128]{3,2,1,0:T(8,128)}), f32[16,3,96,128]{3,2,1,0:T(8,128)}, u32[]{:S(2)}, u32[]{:S(2)}) async-start(f32[16,3,96,128]{3,2,1,0:T(8,128)} %shard_map.56), calls=%async_computation | async-start | bytes 4718592 | tf_op jit(solution)/shard_map/all_to_all | solution.py:258
  11.0 4.3 %shard_map.55 = f32[16,3,96,128]{3,2,1,0:T(8,128)S(1)} custom-call(s32[1]{0:T(128)} %bitcast.block_ref, f32[3,8,96,256]{3,2,1,0:T(8,128)S(1)} %bitcast.59, f32[256,256]{1,0:T(8,128)S(1)} %copy-done.2), custom_call_target="tpu_custom_call" | custom-call | flops 905969664 | bytes 4718592 | tf_op jit(solution)/shard_map/pallas_call | solution.py:131
  16.7 22.5 %all-to-all-done.v_ref = f32[16,3,96,128]{3,2,1,0:T(8,128)} async-done(((f32[16,3,96,128]{3,2,1,0:T(8,128)}), f32[16,3,96,128]{3,2,1,0:T(8,128)}, u32[]{:S(2)}, u32[]{:S(2)}) %all-to-all-start) | async-done | bytes 2359328 | tf_op jit(solution)/shard_map/all_to_all | solution.py:258
  39.3 6.9 %all-to-all-start.1 = ((f32[16,3,96,128]{3,2,1,0:T(8,128)}), f32[16,3,96,128]{3,2,1,0:T(8,128)}, u32[]{:S(2)}, u32[]{:S(2)}) async-start(f32[16,3,96,128]{3,2,1,0:T(8,128)} %copy-done.1), calls=%async_computation.1 | async-start | bytes 4718592 | tf_op jit(solution)/shard_map/all_to_all | solution.py:258
  46.2 1.8 constant_dynamic-slice_fusion
  48.1 2.7 %collective-permute-start.7 = (f32[2,3,96,128]{3,2,1,0:T(8,128)S(1)}, f32[2,3,96,128]{3,2,1,0:T(8,128)S(1)}, u32[]{:S(2)}, u32[]{:S(2)}) collective-permute-start(f32[2,3,96,128]{3,2,1,0:T(8,128)S(1)} %get-tuple-element.39), channel_id=1, source_target_pairs={{0,12},{1,13},{2,14},{3,15},{4,0},{5,1},{6,2},{7,3},{8,4},{9,5},{1... | collective-permute-start | bytes 884744 | tf_op jit(solution)/shard_map/ppermute | solution.py:264
  50.8 2.3 %collective-permute-start.6 = (f32[2,3,96,128]{3,2,1,0:T(8,128)S(1)}, f32[2,3,96,128]{3,2,1,0:T(8,128)S(1)}, u32[]{:S(2)}, u32[]{:S(2)}) collective-permute-start(f32[2,3,96,128]{3,2,1,0:T(8,128)S(1)} %get-tuple-element.42), channel_id=1, source_target_pairs={{0,8},{1,9},{2,10},{3,11},{4,12},{5,13},{6,14},{7,15},{8,0},{9,1},... | collective-permute-start | bytes 884744 | tf_op jit(solution)/shard_map/ppermute | solution.py:264
  53.1 5.4 %collective-permute-start.1 = (f32[4,3,96,128]{3,2,1,0:T(8,128)S(1)}, f32[4,3,96,128]{3,2,1,0:T(8,128)S(1)}, u32[]{:S(2)}, u32[]{:S(2)}) collective-permute-start(f32[4,3,96,128]{3,2,1,0:T(8,128)S(1)} %get-tuple-element.37), channel_id=1, source_target_pairs={{0,3},{1,0},{2,1},{3,2},{4,7},{5,4},{6,5},{7,6},{8,11},{9,8},{10,9... | collective-permute-start | bytes 1769480 | tf_op jit(solution)/shard_map/ppermute | solution.py:263
  58.5 5.2 %collective-permute-done.7 = f32[2,3,96,128]{3,2,1,0:T(8,128)S(1)} collective-permute-done((f32[2,3,96,128]{3,2,1,0:T(8,128)S(1)}, f32[2,3,96,128]{3,2,1,0:T(8,128)S(1)}, u32[]{:S(2)}, u32[]{:S(2)}) %collective-permute-start.7) | collective-permute-done | bytes 294944 | tf_op jit(solution)/shard_map/ppermute | solution.py:264
  63.8 3.4 %collective-permute-done.5 = f32[2,3,96,128]{3,2,1,0:T(8,128)S(1)} collective-permute-done((f32[2,3,96,128]{3,2,1,0:T(8,128)S(1)}, f32[2,3,96,128]{3,2,1,0:T(8,128)S(1)}, u32[]{:S(2)}, u32[]{:S(2)}) %collective-permute-start.5) | collective-permute-done | bytes 294944 | tf_op jit(solution)/shard_map/ppermute | solution.py:264
  69.4 6.3 %collective-permute-start.8 = (f32[4,3,96,128]{3,2,1,0:T(8,128)}, f32[4,3,96,128]{3,2,1,0:T(8,128)S(1)}, u32[]{:S(2)}, u32[]{:S(2)}) collective-permute-start(f32[4,3,96,128]{3,2,1,0:T(8,128)} %pad_maximum_fusion), channel_id=1, source_target_pairs={{0,2},{1,3},{2,0},{3,1},{4,6},{5,7},{6,4},{7,5},{8,10},{9,11},{10,... | collective-permute-start | bytes 1769480 | tf_op jit(solution)/shard_map/ppermute | solution.py:263
  76.0 3.7 %copy-done.4 = f32[1536,1536]{1,0:T(8,128)S(1)} copy-done((f32[1536,1536]{1,0:T(8,128)S(1)}, f32[1536,1536]{1,0:T(8,128)}, u32[]{:S(2)}) %copy-start.4) | copy-done | bytes 9437208
  79.6 14.2 %shard_map.57 = f32[16,3,96,128]{3,2,1,0:T(8,128)S(1)} custom-call(s32[1]{0:T(128)} %bitcast.block_ref, f32[16,3,96,128]{3,2,1,0:T(8,128)} %all-to-all-done.v_ref, f32[1536,1536]{1,0:T(8,128)S(1)} %copy-done.4, f32[1536,128]{1,0:T(8,128)S(1)} %broadcast_in_dim.2.metric_ref), custom_call_target="tpu_custom_call" | custom-call | flops 5435817984 | bytes 14155776 | tf_op jit(solution)/shard_map/pallas_call | solution.py:168
  93.8 10.5 %collective-permute-done = f32[4,3,96,128]{3,2,1,0:T(8,128)S(1)} collective-permute-done((f32[4,3,96,128]{3,2,1,0:T(8,128)S(1)}, f32[4,3,96,128]{3,2,1,0:T(8,128)S(1)}, u32[]{:S(2)}, u32[]{:S(2)}) %collective-permute-start) | collective-permute-done | bytes 589856 | tf_op jit(solution)/shard_map/ppermute | solution.py:263
  105.2 2.9 %collective-permute-start.4 = (f32[2,3,96,128]{3,2,1,0:T(8,128)}, f32[2,3,96,128]{3,2,1,0:T(8,128)}, u32[]{:S(2)}, u32[]{:S(2)}) collective-permute-start(f32[2,3,96,128]{3,2,1,0:T(8,128)} %get-tuple-element.43), channel_id=1, source_target_pairs={{0,12},{1,13},{2,14},{3,15},{4,0},{5,1},{6,2},{7,3},{8,4},{9,5},{1... | collective-permute-start | bytes 884744 | tf_op jit(solution)/shard_map/ppermute | solution.py:264
  108.1 2.2 %collective-permute-start.3 = (f32[2,3,96,128]{3,2,1,0:T(8,128)}, f32[2,3,96,128]{3,2,1,0:T(8,128)}, u32[]{:S(2)}, u32[]{:S(2)}) collective-permute-start(f32[2,3,96,128]{3,2,1,0:T(8,128)} %get-tuple-element.46), channel_id=1, source_target_pairs={{0,8},{1,9},{2,10},{3,11},{4,12},{5,13},{6,14},{7,15},{8,0},{9,1},... | collective-permute-start | bytes 884744 | tf_op jit(solution)/shard_map/ppermute | solution.py:264
  110.3 3.4 %add.184 = f32[16,3,96,128]{3,2,1,0:T(8,128)} add(f32[16,3,96,128]{3,2,1,0:T(8,128)} %all-to-all-done.1, f32[16,3,96,128]{3,2,1,0:T(8,128)S(1)} %shard_map.57) | non-fusion elementwise | flops 589824 | bytes 7077888 | tf_op jit(solution)/shard_map/add | solution.py:286
  113.8 4.8 %collective-permute-done.8 = f32[4,3,96,128]{3,2,1,0:T(8,128)S(1)} collective-permute-done((f32[4,3,96,128]{3,2,1,0:T(8,128)}, f32[4,3,96,128]{3,2,1,0:T(8,128)S(1)}, u32[]{:S(2)}, u32[]{:S(2)}) %collective-permute-start.8) | collective-permute-done | bytes 589856 | tf_op jit(solution)/shard_map/ppermute | solution.py:263
  120.3 3.4 %collective-permute-done.2 = f32[2,3,96,128]{3,2,1,0:T(8,128)} collective-permute-done((f32[2,3,96,128]{3,2,1,0:T(8,128)}, f32[2,3,96,128]{3,2,1,0:T(8,128)}, u32[]{:S(2)}, u32[]{:S(2)}) %collective-permute-start.2) | collective-permute-done | bytes 294944 | tf_op jit(solution)/shard_map/ppermute | solution.py:264
  123.7 11.6 %all-to-all-start.2 = ((f32[16,3,96,128]{3,2,1,0:T(8,128)}), f32[16,3,96,128]{3,2,1,0:T(8,128)S(1)}, u32[]{:S(2)}, u32[]{:S(2)}) async-start(f32[16,3,96,128]{3,2,1,0:T(8,128)} %add.184), calls=%async_computation.2 | async-start | bytes 4718592 | tf_op jit(solution)/shard_map/all_to_all | solution.py:258
  138.8 6.4 %shard_map.58.w_hbm = f32[84,16,96,128]{3,2,1,0:T(8,128)} custom-call(s32[16]{0:T(128)S(1)} %stack.101.at_ref, f32[16,3,96,128]{3,2,1,0:T(8,128)S(1)} %constant_dynamic-update-slice_fusion.v_ref, f32[128,128]{1,0:T(8,128)S(1)} %copy-done.3), custom_call_target="tpu_custom_call" | custom-call | flops 452984832 | bytes 4718592 | tf_op jit(solution)/shard_map/pallas_call | solution.py:214
  145.1 49.6 %all-to-all-done.2.a_ref = f32[16,3,96,128]{3,2,1,0:T(8,128)S(1)} async-done(((f32[16,3,96,128]{3,2,1,0:T(8,128)}), f32[16,3,96,128]{3,2,1,0:T(8,128)S(1)}, u32[]{:S(2)}, u32[]{:S(2)}) %all-to-all-start.2) | async-done | bytes 2359328 | tf_op jit(solution)/shard_map/all_to_all | solution.py:258
  194.8 3.7 %shard_map.59 = f32[3,16,96,128]{3,2,1,0:T(8,128)} custom-call(f32[16,3,96,128]{3,2,1,0:T(8,128)S(1)} %all-to-all-done.2.a_ref, f32[84,16,96,128]{3,2,1,0:T(8,128)} %shard_map.58.w_hbm), custom_call_target="tpu_custom_call" | custom-call | bytes 7077888 | tf_op jit(solution)/shard_map/pallas_call | solution.py:246
  (41 shorter events, 10.0 us)
Async XLA Ops:
  4.4 6.6 %copy-start = (f32[3,8,256,96]{2,3,1,0:T(8,128)S(1)}, f32[3,8,256,96]{2,3,1,0:T(8,128)}, u32[]{:S(2)}) copy-start(f32[3,8,256,96]{2,3,1,0:T(8,128)} %param.5) | copy-start | bytes 7077892
  4.4 6.6 %copy-start.2 = (f32[256,256]{1,0:T(8,128)S(1)}, f32[256,256]{1,0:T(8,128)}, u32[]{:S(2)}) copy-start(f32[256,256]{1,0:T(8,128)} %dx_ref.1) | copy-start | bytes 786436
  4.4 34.8 %all-to-all-start = ((f32[16,3,96,128]{3,2,1,0:T(8,128)}), f32[16,3,96,128]{3,2,1,0:T(8,128)}, u32[]{:S(2)}, u32[]{:S(2)}) async-start(f32[16,3,96,128]{3,2,1,0:T(8,128)} %shard_map.56), calls=%async_computation | async-start | bytes 4718592 | tf_op jit(solution)/shard_map/all_to_all | solution.py:258
  15.3 1.4 copy-start.1
  39.3 71.1 %all-to-all-start.1 = ((f32[16,3,96,128]{3,2,1,0:T(8,128)}), f32[16,3,96,128]{3,2,1,0:T(8,128)}, u32[]{:S(2)}, u32[]{:S(2)}) async-start(f32[16,3,96,128]{3,2,1,0:T(8,128)} %copy-done.1), calls=%async_computation.1 | async-start | bytes 4718592 | tf_op jit(solution)/shard_map/all_to_all | solution.py:258
  48.1 27.6 %copy-start.7 = (f32[1536]{0:T(1024)S(1)}, f32[1536]{0:T(1024)}, u32[]{:S(2)}) copy-start(f32[1536]{0:T(1024)} %param.9) | copy-start | bytes 18436
  48.1 15.7 %collective-permute-start.7 = (f32[2,3,96,128]{3,2,1,0:T(8,128)S(1)}, f32[2,3,96,128]{3,2,1,0:T(8,128)S(1)}, u32[]{:S(2)}, u32[]{:S(2)}) collective-permute-start(f32[2,3,96,128]{3,2,1,0:T(8,128)S(1)} %get-tuple-element.39), channel_id=1, source_target_pairs={{0,12},{1,13},{2,14},{3,15},{4,0},{5,1},{6,2},{7,3},{8,4},{9,5},{1... | collective-permute-start | bytes 884744 | tf_op jit(solution)/shard_map/ppermute | solution.py:264
  50.8 16.3 %collective-permute-start.5 = (f32[2,3,96,128]{3,2,1,0:T(8,128)S(1)}, f32[2,3,96,128]{3,2,1,0:T(8,128)S(1)}, u32[]{:S(2)}, u32[]{:S(2)}) collective-permute-start(f32[2,3,96,128]{3,2,1,0:T(8,128)S(1)} %get-tuple-element.41), channel_id=1, source_target_pairs={{0,4},{1,5},{2,6},{3,7},{4,8},{5,9},{6,10},{7,11},{8,12},{9,13},{1... | collective-permute-start | bytes 884744 | tf_op jit(solution)/shard_map/ppermute | solution.py:264
  50.8 17.0 %collective-permute-start.6 = (f32[2,3,96,128]{3,2,1,0:T(8,128)S(1)}, f32[2,3,96,128]{3,2,1,0:T(8,128)S(1)}, u32[]{:S(2)}, u32[]{:S(2)}) collective-permute-start(f32[2,3,96,128]{3,2,1,0:T(8,128)S(1)} %get-tuple-element.42), channel_id=1, source_target_pairs={{0,8},{1,9},{2,10},{3,11},{4,12},{5,13},{6,14},{7,15},{8,0},{9,1},... | collective-permute-start | bytes 884744 | tf_op jit(solution)/shard_map/ppermute | solution.py:264
  53.1 40.7 %collective-permute-start.1 = (f32[4,3,96,128]{3,2,1,0:T(8,128)S(1)}, f32[4,3,96,128]{3,2,1,0:T(8,128)S(1)}, u32[]{:S(2)}, u32[]{:S(2)}) collective-permute-start(f32[4,3,96,128]{3,2,1,0:T(8,128)S(1)} %get-tuple-element.37), channel_id=1, source_target_pairs={{0,3},{1,0},{2,1},{3,2},{4,7},{5,4},{6,5},{7,6},{8,11},{9,8},{10,9... | collective-permute-start | bytes 1769480 | tf_op jit(solution)/shard_map/ppermute | solution.py:263
  58.5 45.8 %collective-permute-start = (f32[4,3,96,128]{3,2,1,0:T(8,128)S(1)}, f32[4,3,96,128]{3,2,1,0:T(8,128)S(1)}, u32[]{:S(2)}, u32[]{:S(2)}) collective-permute-start(f32[4,3,96,128]{3,2,1,0:T(8,128)S(1)} %get-tuple-element.38), channel_id=1, source_target_pairs={{0,1},{1,2},{2,3},{3,0},{4,5},{5,6},{6,7},{7,4},{8,9},{9,10},{10,1... | collective-permute-start | bytes 1769480 | tf_op jit(solution)/shard_map/ppermute | solution.py:263
  69.4 49.2 %collective-permute-start.8 = (f32[4,3,96,128]{3,2,1,0:T(8,128)}, f32[4,3,96,128]{3,2,1,0:T(8,128)S(1)}, u32[]{:S(2)}, u32[]{:S(2)}) collective-permute-start(f32[4,3,96,128]{3,2,1,0:T(8,128)} %pad_maximum_fusion), channel_id=1, source_target_pairs={{0,2},{1,3},{2,0},{3,1},{4,6},{5,7},{6,4},{7,5},{8,10},{9,11},{10,... | collective-permute-start | bytes 1769480 | tf_op jit(solution)/shard_map/ppermute | solution.py:263
  75.9 3.7 %copy-start.4 = (f32[1536,1536]{1,0:T(8,128)S(1)}, f32[1536,1536]{1,0:T(8,128)}, u32[]{:S(2)}) copy-start(f32[1536,1536]{1,0:T(8,128)} %dy_ref.1) | copy-start | bytes 28311556
  105.2 15.1 %collective-permute-start.4 = (f32[2,3,96,128]{3,2,1,0:T(8,128)}, f32[2,3,96,128]{3,2,1,0:T(8,128)}, u32[]{:S(2)}, u32[]{:S(2)}) collective-permute-start(f32[2,3,96,128]{3,2,1,0:T(8,128)} %get-tuple-element.43), channel_id=1, source_target_pairs={{0,12},{1,13},{2,14},{3,15},{4,0},{5,1},{6,2},{7,3},{8,4},{9,5},{1... | collective-permute-start | bytes 884744 | tf_op jit(solution)/shard_map/ppermute | solution.py:264
  108.1 15.6 %collective-permute-start.2 = (f32[2,3,96,128]{3,2,1,0:T(8,128)}, f32[2,3,96,128]{3,2,1,0:T(8,128)}, u32[]{:S(2)}, u32[]{:S(2)}) collective-permute-start(f32[2,3,96,128]{3,2,1,0:T(8,128)} %get-tuple-element.45), channel_id=1, source_target_pairs={{0,4},{1,5},{2,6},{3,7},{4,8},{5,9},{6,10},{7,11},{8,12},{9,13},{1... | collective-permute-start | bytes 884744 | tf_op jit(solution)/shard_map/ppermute | solution.py:264
  108.1 15.6 %collective-permute-start.3 = (f32[2,3,96,128]{3,2,1,0:T(8,128)}, f32[2,3,96,128]{3,2,1,0:T(8,128)}, u32[]{:S(2)}, u32[]{:S(2)}) collective-permute-start(f32[2,3,96,128]{3,2,1,0:T(8,128)} %get-tuple-element.46), channel_id=1, source_target_pairs={{0,8},{1,9},{2,10},{3,11},{4,12},{5,13},{6,14},{7,15},{8,0},{9,1},... | collective-permute-start | bytes 884744 | tf_op jit(solution)/shard_map/ppermute | solution.py:264
  123.7 71.1 %all-to-all-start.2 = ((f32[16,3,96,128]{3,2,1,0:T(8,128)}), f32[16,3,96,128]{3,2,1,0:T(8,128)S(1)}, u32[]{:S(2)}, u32[]{:S(2)}) async-start(f32[16,3,96,128]{3,2,1,0:T(8,128)} %add.184), calls=%async_computation.2 | async-start | bytes 4718592 | tf_op jit(solution)/shard_map/all_to_all | solution.py:258
  135.5 3.1 %copy-start.5 = (f32[3,96,128]{2,1,0:T(8,128)S(1)}, f32[3,96,128]{2,1,0:T(8,128)}, u32[]{:S(2)}) copy-start(f32[3,96,128]{2,1,0:T(8,128)} %get-tuple-element.31) | copy-start | bytes 442372
  135.5 3.1 %copy-start.6 = (f32[3,96,128]{2,1,0:T(8,128)S(1)}, f32[3,96,128]{2,1,0:T(8,128)}, u32[]{:S(2)}) copy-start(f32[3,96,128]{2,1,0:T(8,128)} %get-tuple-element.32) | copy-start | bytes 442372
  135.5 3.2 %copy-start.3 = (f32[128,128]{1,0:T(8,128)S(1)}, f32[128,128]{1,0:T(8,128)}, u32[]{:S(2)}) copy-start(f32[128,128]{1,0:T(8,128)} %dz_ref.1) | copy-start | bytes 196612

commit v6 on v5

--- a/solution.py
+++ b/solution.py
@@ -34,17 +34,19 @@
     return ((lane & 7) << 4) | (lane & 8) | (lane >> 4)
 
 
-def over_rows(components, body):
-    tiles = YB // 8
+def over_rows(components, body, first=0, count=YB):
+    tiles = count // 8
 
     def step(i, _):
-        body(components[0] + i // tiles, pl.ds(pl.multiple_of(i % tiles * 8, 8), 8))
+        body(components[0] + i // tiles, pl.ds(pl.multiple_of(first + i % tiles * 8, 8), 8))
         return 0
 
     lax.fori_loop(0, len(components) * tiles, step, 0, unroll=3)
 
 
 ALL = range(NC)
+HALF = YB // 2
+HALVES = [(c, first) for c in ALL for first in (0, HALF)]
 
 
 def split(v):
@@ -74,8 +76,11 @@
 
 def pack_kernel(v_hbm, out_hbm, v_ref, out_ref, sems):
     lane = lanes8()
-    loads = [pltpu.make_async_copy(v_hbm.at[c], v_ref.at[c], sems.at[c]) for c in ALL]
-    stores = [pltpu.make_async_copy(out_ref.at[c], out_hbm.at[:, c], sems.at[NC + c]) for c in ALL]
+    loads, stores = [], []
+    for i, (c, first) in enumerate(HALVES):
+        rows = pl.ds(first, HALF)
+        loads.append(pltpu.make_async_copy(v_hbm.at[c, :, rows], v_ref.at[c, :, rows], sems.at[i]))
+        stores.append(pltpu.make_async_copy(out_ref.at[c, :, rows], out_hbm.at[:, c, rows], sems.at[len(HALVES) + i]))
     for load in loads:
         load.start()
 
@@ -85,10 +90,10 @@
             for i in range(8):
                 out_ref[c, half * 8 + i, rows, :] = arrs[i]
 
-    for c in ALL:
-        loads[c].wait()
-        over_rows([c], body)
-        stores[c].start()
+    for i, (c, first) in enumerate(HALVES):
+        loads[i].wait()
+        over_rows([c], body, first, HALF)
+        stores[i].start()
     for store in stores:
         store.wait()
 
@@ -105,7 +110,7 @@
         scratch_shapes=[
             pltpu.VMEM((NC, ZB, YB, NX), jnp.float32),
             pltpu.VMEM((NC, NB, YB, LN), jnp.float32),
-            pltpu.SemaphoreType.DMA((2 * NC,)),
+            pltpu.SemaphoreType.DMA((2 * len(HALVES),)),
         ],
     )(v)
 
@@ -224,8 +229,11 @@
 
 def finish_kernel(a_ref, w_hbm, out_hbm, w_ref, sems):
     lane = lanes8()
-    loads = [pltpu.make_async_copy(w_hbm.at[c], w_ref.at[c], sems.at[c]) for c in ALL]
-    stores = [pltpu.make_async_copy(w_ref.at[c], out_hbm.at[c], sems.at[NC + c]) for c in ALL]
+    loads, stores = [], []
+    for i, (c, first) in enumerate(HALVES):
+        rows = pl.ds(first, HALF)
+        loads.append(pltpu.make_async_copy(w_hbm.at[c, :, rows], w_ref.at[c, :, rows], sems.at[i]))
+        stores.append(pltpu.make_async_copy(w_ref.at[c, :, rows], out_hbm.at[c, :, rows], sems.at[len(HALVES) + i]))
     for load in loads:
         load.start()
 
@@ -234,10 +242,10 @@
         for x in range(NB):
             w_ref[c, x, rows, :] += arrs[x]
 
-    for c in ALL:
-        loads[c].wait()
-        over_rows([c], body)
-        stores[c].start()
+    for i, (c, first) in enumerate(HALVES):
+        loads[i].wait()
+        over_rows([c], body, first, HALF)
+        stores[i].start()
     for store in stores:
         store.wait()
 
@@ -250,7 +258,7 @@
         in_specs=[VMEM, HBM],
         out_specs=HBM,
         out_shape=PENCILS,
-        scratch_shapes=[pltpu.VMEM(PENCILS.shape, jnp.float32), pltpu.SemaphoreType.DMA((2 * NC,))],
+        scratch_shapes=[pltpu.VMEM(PENCILS.shape, jnp.float32), pltpu.SemaphoreType.DMA((2 * len(HALVES),))],
     )(accum_z, term_z)
 
 

time: 199 us -> 199 us (level)
  no operation moved by 1% of the time
where the time goes in v6:
time: 199 us; the launch traced here: 198 us
  waiting for transfers between devices  101 us (51%)
  starting transfers between devices  47 us (24%)
  Pallas kernels  32.5 us (16%)
  local copies, waits for them, and re-layouts  11.8 us (6%)
  other arithmetic  5.33 us (3%)
    all_to_all x3, waiting for transfers between devices, exchange(): return lax.all_to_all(a, axis, split_axis=0, concat_axis=0, tiled=True)  72.2 us
    all_to_all x3, starting transfers between devices, exchange(): return lax.all_to_all(a, axis, split_axis=0, concat_axis=0, tiled=True)  25.2 us
    ppermute x3, waiting for transfers between devices, col_exchange(): lax.ppermute(x, 'col', [(i * 4 + j, i * 4 + (j + s) % 4) for i in range(4...  15.3 us
    pallas_call x1, Pallas kernels, y_term(): call(y_kernel, 6 * NY * NY * NC * LN, 2 * SIZE + NY * NY * 4, grid=(NB //...  14.2 us
    ppermute x6, waiting for transfers between devices, col_exchange(): lax.ppermute(x, 'col', [(i * 4 + j, (i + s) % 4 * 4 + j) for i in range(4...  13.7 us
    ppermute x3, starting transfers between devices, col_exchange(): lax.ppermute(x, 'col', [(i * 4 + j, i * 4 + (j + s) % 4) for i in range(4...  11.7 us
    ppermute x6, starting transfers between devices, col_exchange(): lax.ppermute(x, 'col', [(i * 4 + j, (i + s) % 4 * 4 + j) for i in range(4...  10.2 us
    unnamed x24, local copies, waits for them, and re-layouts  8.21 us
  transfers between devices with their start and end apart: 12, of which 8 were waited for; matrix products, arithmetic and copies ran while one was open for 6% of the time, Pallas kernels for 13%

profile of v6, /device:TPU:4, one launch (start us, length us, event | category | flops | bytes accessed | tf_op | source)
XLA Modules:
  0.0 198.1 jit_solution(9640401261282085581)
XLA Ops:
  0.0 4.2 %shard_map.56 = f32[16,3,96,128]{3,2,1,0:T(8,128)} custom-call(f32[3,8,96,256]{3,2,1,0:T(8,128)} %bitcast.58), custom_call_target="tpu_custom_call" | custom-call | bytes 4718592 | tf_op jit(solution)/shard_map/pallas_call | solution.py:102
  4.2 6.6 %all-to-all-start = ((f32[16,3,96,128]{3,2,1,0:T(8,128)}), f32[16,3,96,128]{3,2,1,0:T(8,128)}, u32[]{:S(2)}, u32[]{:S(2)}) async-start(f32[16,3,96,128]{3,2,1,0:T(8,128)} %shard_map.56), calls=%async_computation | async-start | bytes 4718592 | tf_op jit(solution)/shard_map/all_to_all | solution.py:266
  10.9 4.3 %shard_map.55 = f32[16,3,96,128]{3,2,1,0:T(8,128)S(1)} custom-call(s32[1]{0:T(128)} %bitcast.block_ref, f32[3,8,96,256]{3,2,1,0:T(8,128)S(1)} %bitcast.59, f32[256,256]{1,0:T(8,128)S(1)} %copy-done.2), custom_call_target="tpu_custom_call" | custom-call | flops 905969664 | bytes 4718592 | tf_op jit(solution)/shard_map/pallas_call | solution.py:136
  16.6 22.5 %all-to-all-done.v_ref = f32[16,3,96,128]{3,2,1,0:T(8,128)} async-done(((f32[16,3,96,128]{3,2,1,0:T(8,128)}), f32[16,3,96,128]{3,2,1,0:T(8,128)}, u32[]{:S(2)}, u32[]{:S(2)}) %all-to-all-start) | async-done | bytes 2359328 | tf_op jit(solution)/shard_map/all_to_all | solution.py:266
  39.1 6.9 %all-to-all-start.1 = ((f32[16,3,96,128]{3,2,1,0:T(8,128)}), f32[16,3,96,128]{3,2,1,0:T(8,128)}, u32[]{:S(2)}, u32[]{:S(2)}) async-start(f32[16,3,96,128]{3,2,1,0:T(8,128)} %copy-done.1), calls=%async_computation.1 | async-start | bytes 4718592 | tf_op jit(solution)/shard_map/all_to_all | solution.py:266
  46.0 1.8 constant_dynamic-slice_fusion
  47.9 2.7 %collective-permute-start.7 = (f32[2,3,96,128]{3,2,1,0:T(8,128)S(1)}, f32[2,3,96,128]{3,2,1,0:T(8,128)S(1)}, u32[]{:S(2)}, u32[]{:S(2)}) collective-permute-start(f32[2,3,96,128]{3,2,1,0:T(8,128)S(1)} %get-tuple-element.39), channel_id=1, source_target_pairs={{0,12},{1,13},{2,14},{3,15},{4,0},{5,1},{6,2},{7,3},{8,4},{9,5},{1... | collective-permute-start | bytes 884744 | tf_op jit(solution)/shard_map/ppermute | solution.py:272
  50.7 2.3 %collective-permute-start.6 = (f32[2,3,96,128]{3,2,1,0:T(8,128)S(1)}, f32[2,3,96,128]{3,2,1,0:T(8,128)S(1)}, u32[]{:S(2)}, u32[]{:S(2)}) collective-permute-start(f32[2,3,96,128]{3,2,1,0:T(8,128)S(1)} %get-tuple-element.42), channel_id=1, source_target_pairs={{0,8},{1,9},{2,10},{3,11},{4,12},{5,13},{6,14},{7,15},{8,0},{9,1},... | collective-permute-start | bytes 884744 | tf_op jit(solution)/shard_map/ppermute | solution.py:272
  53.0 5.4 %collective-permute-start.1 = (f32[4,3,96,128]{3,2,1,0:T(8,128)S(1)}, f32[4,3,96,128]{3,2,1,0:T(8,128)S(1)}, u32[]{:S(2)}, u32[]{:S(2)}) collective-permute-start(f32[4,3,96,128]{3,2,1,0:T(8,128)S(1)} %get-tuple-element.37), channel_id=1, source_target_pairs={{0,3},{1,0},{2,1},{3,2},{4,7},{5,4},{6,5},{7,6},{8,11},{9,8},{10,9... | collective-permute-start | bytes 1769480 | tf_op jit(solution)/shard_map/ppermute | solution.py:271
  58.4 5.2 %collective-permute-done.7 = f32[2,3,96,128]{3,2,1,0:T(8,128)S(1)} collective-permute-done((f32[2,3,96,128]{3,2,1,0:T(8,128)S(1)}, f32[2,3,96,128]{3,2,1,0:T(8,128)S(1)}, u32[]{:S(2)}, u32[]{:S(2)}) %collective-permute-start.7) | collective-permute-done | bytes 294944 | tf_op jit(solution)/shard_map/ppermute | solution.py:272
  63.6 3.4 %collective-permute-done.5 = f32[2,3,96,128]{3,2,1,0:T(8,128)S(1)} collective-permute-done((f32[2,3,96,128]{3,2,1,0:T(8,128)S(1)}, f32[2,3,96,128]{3,2,1,0:T(8,128)S(1)}, u32[]{:S(2)}, u32[]{:S(2)}) %collective-permute-start.5) | collective-permute-done | bytes 294944 | tf_op jit(solution)/shard_map/ppermute | solution.py:272
  69.2 6.3 %collective-permute-start.8 = (f32[4,3,96,128]{3,2,1,0:T(8,128)}, f32[4,3,96,128]{3,2,1,0:T(8,128)S(1)}, u32[]{:S(2)}, u32[]{:S(2)}) collective-permute-start(f32[4,3,96,128]{3,2,1,0:T(8,128)} %pad_maximum_fusion), channel_id=1, source_target_pairs={{0,2},{1,3},{2,0},{3,1},{4,6},{5,7},{6,4},{7,5},{8,10},{9,11},{10,... | collective-permute-start | bytes 1769480 | tf_op jit(solution)/shard_map/ppermute | solution.py:271
  75.8 3.7 %copy-done.4 = f32[1536,1536]{1,0:T(8,128)S(1)} copy-done((f32[1536,1536]{1,0:T(8,128)S(1)}, f32[1536,1536]{1,0:T(8,128)}, u32[]{:S(2)}) %copy-start.4) | copy-done | bytes 9437208
  79.5 14.2 %shard_map.57 = f32[16,3,96,128]{3,2,1,0:T(8,128)S(1)} custom-call(s32[1]{0:T(128)} %bitcast.block_ref, f32[16,3,96,128]{3,2,1,0:T(8,128)} %all-to-all-done.v_ref, f32[1536,1536]{1,0:T(8,128)S(1)} %copy-done.4, f32[1536,128]{1,0:T(8,128)S(1)} %broadcast_in_dim.2.metric_ref), custom_call_target="tpu_custom_call" | custom-call | flops 5435817984 | bytes 14155776 | tf_op jit(solution)/shard_map/pallas_call | solution.py:173
  93.7 10.5 %collective-permute-done = f32[4,3,96,128]{3,2,1,0:T(8,128)S(1)} collective-permute-done((f32[4,3,96,128]{3,2,1,0:T(8,128)S(1)}, f32[4,3,96,128]{3,2,1,0:T(8,128)S(1)}, u32[]{:S(2)}, u32[]{:S(2)}) %collective-permute-start) | collective-permute-done | bytes 589856 | tf_op jit(solution)/shard_map/ppermute | solution.py:271
  105.1 2.9 %collective-permute-start.4 = (f32[2,3,96,128]{3,2,1,0:T(8,128)}, f32[2,3,96,128]{3,2,1,0:T(8,128)}, u32[]{:S(2)}, u32[]{:S(2)}) collective-permute-start(f32[2,3,96,128]{3,2,1,0:T(8,128)} %get-tuple-element.43), channel_id=1, source_target_pairs={{0,12},{1,13},{2,14},{3,15},{4,0},{5,1},{6,2},{7,3},{8,4},{9,5},{1... | collective-permute-start | bytes 884744 | tf_op jit(solution)/shard_map/ppermute | solution.py:272
  108.0 2.2 %collective-permute-start.3 = (f32[2,3,96,128]{3,2,1,0:T(8,128)}, f32[2,3,96,128]{3,2,1,0:T(8,128)}, u32[]{:S(2)}, u32[]{:S(2)}) collective-permute-start(f32[2,3,96,128]{3,2,1,0:T(8,128)} %get-tuple-element.46), channel_id=1, source_target_pairs={{0,8},{1,9},{2,10},{3,11},{4,12},{5,13},{6,14},{7,15},{8,0},{9,1},... | collective-permute-start | bytes 884744 | tf_op jit(solution)/shard_map/ppermute | solution.py:272
  110.2 3.4 %add.184 = f32[16,3,96,128]{3,2,1,0:T(8,128)} add(f32[16,3,96,128]{3,2,1,0:T(8,128)} %all-to-all-done.1, f32[16,3,96,128]{3,2,1,0:T(8,128)S(1)} %shard_map.57) | non-fusion elementwise | flops 589824 | bytes 7077888 | tf_op jit(solution)/shard_map/add | solution.py:294
  113.6 4.8 %collective-permute-done.8 = f32[4,3,96,128]{3,2,1,0:T(8,128)S(1)} collective-permute-done((f32[4,3,96,128]{3,2,1,0:T(8,128)}, f32[4,3,96,128]{3,2,1,0:T(8,128)S(1)}, u32[]{:S(2)}, u32[]{:S(2)}) %collective-permute-start.8) | collective-permute-done | bytes 589856 | tf_op jit(solution)/shard_map/ppermute | solution.py:271
  120.1 3.4 %collective-permute-done.2 = f32[2,3,96,128]{3,2,1,0:T(8,128)} collective-permute-done((f32[2,3,96,128]{3,2,1,0:T(8,128)}, f32[2,3,96,128]{3,2,1,0:T(8,128)}, u32[]{:S(2)}, u32[]{:S(2)}) %collective-permute-start.2) | collective-permute-done | bytes 294944 | tf_op jit(solution)/shard_map/ppermute | solution.py:272
  123.6 11.6 %all-to-all-start.2 = ((f32[16,3,96,128]{3,2,1,0:T(8,128)}), f32[16,3,96,128]{3,2,1,0:T(8,128)S(1)}, u32[]{:S(2)}, u32[]{:S(2)}) async-start(f32[16,3,96,128]{3,2,1,0:T(8,128)} %add.184), calls=%async_computation.2 | async-start | bytes 4718592 | tf_op jit(solution)/shard_map/all_to_all | solution.py:266
  138.6 6.4 %shard_map.58.w_hbm = f32[84,16,96,128]{3,2,1,0:T(8,128)} custom-call(s32[16]{0:T(128)S(1)} %stack.101.at_ref, f32[16,3,96,128]{3,2,1,0:T(8,128)S(1)} %constant_dynamic-update-slice_fusion.v_ref, f32[128,128]{1,0:T(8,128)S(1)} %copy-done.3), custom_call_target="tpu_custom_call" | custom-call | flops 452984832 | bytes 4718592 | tf_op jit(solution)/shard_map/pallas_call | solution.py:219
  145.0 49.6 %all-to-all-done.2.a_ref = f32[16,3,96,128]{3,2,1,0:T(8,128)S(1)} async-done(((f32[16,3,96,128]{3,2,1,0:T(8,128)}), f32[16,3,96,128]{3,2,1,0:T(8,128)S(1)}, u32[]{:S(2)}, u32[]{:S(2)}) %all-to-all-start.2) | async-done | bytes 2359328 | tf_op jit(solution)/shard_map/all_to_all | solution.py:266
  194.6 3.5 %shard_map.59 = f32[3,16,96,128]{3,2,1,0:T(8,128)} custom-call(f32[16,3,96,128]{3,2,1,0:T(8,128)S(1)} %all-to-all-done.2.a_ref, f32[84,16,96,128]{3,2,1,0:T(8,128)} %shard_map.58.w_hbm), custom_call_target="tpu_custom_call" | custom-call | bytes 7077888 | tf_op jit(solution)/shard_map/pallas_call | solution.py:254
  (41 shorter events, 10.0 us)
Async XLA Ops:
  4.2 6.6 %copy-start = (f32[3,8,256,96]{2,3,1,0:T(8,128)S(1)}, f32[3,8,256,96]{2,3,1,0:T(8,128)}, u32[]{:S(2)}) copy-start(f32[3,8,256,96]{2,3,1,0:T(8,128)} %param.5) | copy-start | bytes 7077892
  4.2 6.6 %copy-start.2 = (f32[256,256]{1,0:T(8,128)S(1)}, f32[256,256]{1,0:T(8,128)}, u32[]{:S(2)}) copy-start(f32[256,256]{1,0:T(8,128)} %dx_ref.1) | copy-start | bytes 786436
  4.2 34.8 %all-to-all-start = ((f32[16,3,96,128]{3,2,1,0:T(8,128)}), f32[16,3,96,128]{3,2,1,0:T(8,128)}, u32[]{:S(2)}, u32[]{:S(2)}) async-start(f32[16,3,96,128]{3,2,1,0:T(8,128)} %shard_map.56), calls=%async_computation | async-start | bytes 4718592 | tf_op jit(solution)/shard_map/all_to_all | solution.py:266
  15.2 1.4 copy-start.1
  39.1 71.1 %all-to-all-start.1 = ((f32[16,3,96,128]{3,2,1,0:T(8,128)}), f32[16,3,96,128]{3,2,1,0:T(8,128)}, u32[]{:S(2)}, u32[]{:S(2)}) async-start(f32[16,3,96,128]{3,2,1,0:T(8,128)} %copy-done.1), calls=%async_computation.1 | async-start | bytes 4718592 | tf_op jit(solution)/shard_map/all_to_all | solution.py:266
  47.9 27.6 %copy-start.7 = (f32[1536]{0:T(1024)S(1)}, f32[1536]{0:T(1024)}, u32[]{:S(2)}) copy-start(f32[1536]{0:T(1024)} %param.9) | copy-start | bytes 18436
  47.9 15.7 %collective-permute-start.7 = (f32[2,3,96,128]{3,2,1,0:T(8,128)S(1)}, f32[2,3,96,128]{3,2,1,0:T(8,128)S(1)}, u32[]{:S(2)}, u32[]{:S(2)}) collective-permute-start(f32[2,3,96,128]{3,2,1,0:T(8,128)S(1)} %get-tuple-element.39), channel_id=1, source_target_pairs={{0,12},{1,13},{2,14},{3,15},{4,0},{5,1},{6,2},{7,3},{8,4},{9,5},{1... | collective-permute-start | bytes 884744 | tf_op jit(solution)/shard_map/ppermute | solution.py:272
  50.6 16.3 %collective-permute-start.5 = (f32[2,3,96,128]{3,2,1,0:T(8,128)S(1)}, f32[2,3,96,128]{3,2,1,0:T(8,128)S(1)}, u32[]{:S(2)}, u32[]{:S(2)}) collective-permute-start(f32[2,3,96,128]{3,2,1,0:T(8,128)S(1)} %get-tuple-element.41), channel_id=1, source_target_pairs={{0,4},{1,5},{2,6},{3,7},{4,8},{5,9},{6,10},{7,11},{8,12},{9,13},{1... | collective-permute-start | bytes 884744 | tf_op jit(solution)/shard_map/ppermute | solution.py:272
  50.7 17.0 %collective-permute-start.6 = (f32[2,3,96,128]{3,2,1,0:T(8,128)S(1)}, f32[2,3,96,128]{3,2,1,0:T(8,128)S(1)}, u32[]{:S(2)}, u32[]{:S(2)}) collective-permute-start(f32[2,3,96,128]{3,2,1,0:T(8,128)S(1)} %get-tuple-element.42), channel_id=1, source_target_pairs={{0,8},{1,9},{2,10},{3,11},{4,12},{5,13},{6,14},{7,15},{8,0},{9,1},... | collective-permute-start | bytes 884744 | tf_op jit(solution)/shard_map/ppermute | solution.py:272
  53.0 40.7 %collective-permute-start.1 = (f32[4,3,96,128]{3,2,1,0:T(8,128)S(1)}, f32[4,3,96,128]{3,2,1,0:T(8,128)S(1)}, u32[]{:S(2)}, u32[]{:S(2)}) collective-permute-start(f32[4,3,96,128]{3,2,1,0:T(8,128)S(1)} %get-tuple-element.37), channel_id=1, source_target_pairs={{0,3},{1,0},{2,1},{3,2},{4,7},{5,4},{6,5},{7,6},{8,11},{9,8},{10,9... | collective-permute-start | bytes 1769480 | tf_op jit(solution)/shard_map/ppermute | solution.py:271
  58.4 45.8 %collective-permute-start = (f32[4,3,96,128]{3,2,1,0:T(8,128)S(1)}, f32[4,3,96,128]{3,2,1,0:T(8,128)S(1)}, u32[]{:S(2)}, u32[]{:S(2)}) collective-permute-start(f32[4,3,96,128]{3,2,1,0:T(8,128)S(1)} %get-tuple-element.38), channel_id=1, source_target_pairs={{0,1},{1,2},{2,3},{3,0},{4,5},{5,6},{6,7},{7,4},{8,9},{9,10},{10,1... | collective-permute-start | bytes 1769480 | tf_op jit(solution)/shard_map/ppermute | solution.py:271
  69.2 49.2 %collective-permute-start.8 = (f32[4,3,96,128]{3,2,1,0:T(8,128)}, f32[4,3,96,128]{3,2,1,0:T(8,128)S(1)}, u32[]{:S(2)}, u32[]{:S(2)}) collective-permute-start(f32[4,3,96,128]{3,2,1,0:T(8,128)} %pad_maximum_fusion), channel_id=1, source_target_pairs={{0,2},{1,3},{2,0},{3,1},{4,6},{5,7},{6,4},{7,5},{8,10},{9,11},{10,... | collective-permute-start | bytes 1769480 | tf_op jit(solution)/shard_map/ppermute | solution.py:271
  75.8 3.7 %copy-start.4 = (f32[1536,1536]{1,0:T(8,128)S(1)}, f32[1536,1536]{1,0:T(8,128)}, u32[]{:S(2)}) copy-start(f32[1536,1536]{1,0:T(8,128)} %dy_ref.1) | copy-start | bytes 28311556
  105.1 15.1 %collective-permute-start.4 = (f32[2,3,96,128]{3,2,1,0:T(8,128)}, f32[2,3,96,128]{3,2,1,0:T(8,128)}, u32[]{:S(2)}, u32[]{:S(2)}) collective-permute-start(f32[2,3,96,128]{3,2,1,0:T(8,128)} %get-tuple-element.43), channel_id=1, source_target_pairs={{0,12},{1,13},{2,14},{3,15},{4,0},{5,1},{6,2},{7,3},{8,4},{9,5},{1... | collective-permute-start | bytes 884744 | tf_op jit(solution)/shard_map/ppermute | solution.py:272
  108.0 15.6 %collective-permute-start.2 = (f32[2,3,96,128]{3,2,1,0:T(8,128)}, f32[2,3,96,128]{3,2,1,0:T(8,128)}, u32[]{:S(2)}, u32[]{:S(2)}) collective-permute-start(f32[2,3,96,128]{3,2,1,0:T(8,128)} %get-tuple-element.45), channel_id=1, source_target_pairs={{0,4},{1,5},{2,6},{3,7},{4,8},{5,9},{6,10},{7,11},{8,12},{9,13},{1... | collective-permute-start | bytes 884744 | tf_op jit(solution)/shard_map/ppermute | solution.py:272
  108.0 15.6 %collective-permute-start.3 = (f32[2,3,96,128]{3,2,1,0:T(8,128)}, f32[2,3,96,128]{3,2,1,0:T(8,128)}, u32[]{:S(2)}, u32[]{:S(2)}) collective-permute-start(f32[2,3,96,128]{3,2,1,0:T(8,128)} %get-tuple-element.46), channel_id=1, source_target_pairs={{0,8},{1,9},{2,10},{3,11},{4,12},{5,13},{6,14},{7,15},{8,0},{9,1},... | collective-permute-start | bytes 884744 | tf_op jit(solution)/shard_map/ppermute | solution.py:272
  123.6 71.1 %all-to-all-start.2 = ((f32[16,3,96,128]{3,2,1,0:T(8,128)}), f32[16,3,96,128]{3,2,1,0:T(8,128)S(1)}, u32[]{:S(2)}, u32[]{:S(2)}) async-start(f32[16,3,96,128]{3,2,1,0:T(8,128)} %add.184), calls=%async_computation.2 | async-start | bytes 4718592 | tf_op jit(solution)/shard_map/all_to_all | solution.py:266
  135.4 3.1 %copy-start.5 = (f32[3,96,128]{2,1,0:T(8,128)S(1)}, f32[3,96,128]{2,1,0:T(8,128)}, u32[]{:S(2)}) copy-start(f32[3,96,128]{2,1,0:T(8,128)} %get-tuple-element.31) | copy-start | bytes 442372
  135.4 3.1 %copy-start.6 = (f32[3,96,128]{2,1,0:T(8,128)S(1)}, f32[3,96,128]{2,1,0:T(8,128)}, u32[]{:S(2)}) copy-start(f32[3,96,128]{2,1,0:T(8,128)} %get-tuple-element.32) | copy-start | bytes 442372
  135.4 3.2 %copy-start.3 = (f32[128,128]{1,0:T(8,128)S(1)}, f32[128,128]{1,0:T(8,128)}, u32[]{:S(2)}) copy-start(f32[128,128]{1,0:T(8,128)} %dz_ref.1) | copy-start | bytes 196612
